TPU v7x, 32 devices: a whole 2x2x4 slice. The times are simulated.
32 devices in a mesh: rep: 8 (over y, x, core), shard: 4 (over z).
Axes of the slice: x: 2, y: 2, z: 4, core: 2. Of those that a mesh axis runs over, the one named last changes fastest.
Arguments:
- tokens: bfloat16 [16384, 1024], P(('rep', 'shard')), may hold values from -6 to 6
- doc_ids: int32 [16384], P(('rep', 'shard')), may hold values from 0 to 511, as said below
- routes: int32 [16384, 8], P(('rep', 'shard')), may hold values from 0 to 15, all different within a row; in each aligned block of 512 rows (0 to 511, 512 to 1023, ...) at most 288 rows name the same one
- norm_in_gain: bfloat16 [1024], P('shard'), may hold values from 0.5 to 1.5
- w_query: bfloat16 [1024, 1024], P('shard'), may hold values from -0.1875 to 0.1875
- w_key: bfloat16 [1024, 512], P('shard'), may hold values from -0.1875 to 0.1875
- w_value: bfloat16 [1024, 512], P('shard'), may hold values from -0.1875 to 0.1875
- w_out: bfloat16 [1024, 1024], P('shard'), may hold values from -0.75 to 0.75
- norm_mid_gain: bfloat16 [1024], P('shard'), may hold values from 0.5 to 1.5
- w_router: bfloat16 [1024, 16], P('shard'), may hold values from -0.09375 to 0.09375
- w_expert_in: bfloat16 [16, 1024, 1024], P('shard'), may hold values from -0.1875 to 0.1875
- w_expert_down: bfloat16 [16, 512, 1024], P('shard'), may hold values from -0.75 to 0.75
- cotangent: bfloat16 [16384, 1024], P(('rep', 'shard')), may hold values from -6 to 6
Outputs:
- mixed: bfloat16 [16384, 1024], P(('rep', 'shard'))
- grad_tokens: float32 [16384, 1024], P(('rep', 'shard'))
- grad_norm_in_gain: float32 [1024], P('shard')
- grad_w_query: float32 [1024, 1024], P('shard')
- grad_w_key: float32 [1024, 512], P('shard')
- grad_w_value: float32 [1024, 512], P('shard')
- grad_w_out: float32 [1024, 1024], P('shard')
- grad_norm_mid_gain: float32 [1024], P('shard')
- grad_w_router: float32 [1024, 16], P('shard')
- grad_w_expert_in: float32 [16, 1024, 1024], P('shard')
- grad_w_expert_down: float32 [16, 512, 1024], P('shard')
Inputs may be any that keep to these rules, and one draw needn't show every extreme that they name: `doc_ids`: in every aligned block of 512 tokens the numbers start at 0 and rise by 0 or 1 from token to token. Among the 512 tokens of one device, no expert is named by more than 288 routes.
All inputs are finite; a program needn't handle non-finite values.
Results may differ from a plain program's by a relative error of at most 0.019.
Values may be sent and summed in bfloat16 or wider, within the bound.
A program may use at most 320 MiB of HBM per device.

v0:
```python
import jax
import jax.numpy as jnp
from jax import lax
from jax.sharding import PartitionSpec as P

HEADS = 16
KV_HEADS = 8
HEAD_DIM = 64
EXPERTS = 16
TOP_K = 8
CAP = 288


epsilon = 1e-06
rope_base = 10000.0
masked_score = -1e30


def positions(doc_rows):
    row_count = doc_rows.shape[0]
    places = jnp.arange(row_count, dtype=jnp.int32)
    opening = jnp.concatenate([jnp.ones((1,), dtype=jnp.bool_), doc_rows[1:] != doc_rows[:-1]])
    begins = lax.cummax(jnp.where(opening, places, 0), axis=0)
    return places - begins


def rotary_tables(places, head_width):
    half_width = head_width // 2
    frequencies = jnp.power(
        rope_base, -2.0 * jnp.arange(half_width, dtype=jnp.float32) / head_width
    )
    angles = places.astype(jnp.float32)[:, None] * frequencies[None, :]
    return (jnp.cos(angles)[:, None, :], jnp.sin(angles)[:, None, :])


def rotate(values, cosine, sine_table):
    half_width = values.shape[-1] // 2
    former, latter = (values[..., :half_width], values[..., half_width:])
    return jnp.concatenate(
        [former * cosine - latter * sine_table, latter * cosine + former * sine_table], axis=-1
    )


def unrotate(values, cosine, sine_table):
    half_width = values.shape[-1] // 2
    former, latter = (values[..., :half_width], values[..., half_width:])
    return jnp.concatenate(
        [former * cosine + latter * sine_table, latter * cosine - former * sine_table], axis=-1
    )


def normalize(values):
    row_scale = lax.rsqrt(jnp.mean(values * values, axis=-1, keepdims=True) + epsilon)
    return (values * row_scale, row_scale)


def norm_back(grad_scaled, normed, row_scale, gain_full):
    grad_normed = grad_scaled * gain_full
    inner = jnp.mean(grad_normed * normed, axis=-1, keepdims=True)
    return (row_scale * (grad_normed - normed * inner), jnp.sum(grad_scaled * normed, axis=0))


def dispatch(route_rows):
    flat_routes = route_rows.reshape(-1)
    route_count = flat_routes.shape[0]
    onehot = (flat_routes[:, None] == jnp.arange(EXPERTS, dtype=jnp.int32)[None, :]).astype(
        jnp.int32
    )
    expert_rank = jnp.sum((jnp.cumsum(onehot, axis=0) - 1) * onehot, axis=1)
    slot_index = flat_routes * CAP + expert_rank
    source = (
        jnp.full((EXPERTS * CAP,), route_count, dtype=jnp.int32)
        .at[slot_index]
        .set(jnp.arange(route_count, dtype=jnp.int32))
    )
    filled = source < route_count
    token_of = jnp.where(filled, source // TOP_K, 0)
    route_of = jnp.where(filled, source, 0)
    return (token_of, route_of, filled)


def score_block(query_blk, key_part, doc_query, doc_key):
    scores = jnp.einsum(
        "qgrd,kgd->grqk", query_blk, key_part, preferred_element_type=jnp.float32
    ) * query_blk.shape[-1] ** (-0.5)
    query_place = jnp.arange(query_blk.shape[0], dtype=jnp.int32)
    key_place = jnp.arange(key_part.shape[0], dtype=jnp.int32)
    allowed = (doc_query[:, None] == doc_key[None, :]) & (
        query_place[:, None] >= key_place[None, :]
    )
    return jnp.where(allowed, scores, masked_score)


def attend(query_rows, key_rows, value_rows, doc_rows):
    scores = score_block(query_rows, key_rows, doc_rows, doc_rows)
    row_max = jnp.max(scores, axis=-1, keepdims=True)
    exponent = jnp.exp(scores - row_max)
    row_total = jnp.sum(exponent, axis=-1, keepdims=True)
    probs_low = (exponent / row_total).astype(jnp.bfloat16)
    outputs = jnp.einsum(
        "grqk,kgd->qgrd", probs_low, value_rows, preferred_element_type=jnp.float32
    ).astype(jnp.bfloat16)
    lse_parts = row_max + jnp.log(row_total)
    return (outputs, lse_parts)


def attend_back(query_rows, key_rows, value_rows, doc_rows, log_sums, grad_att):
    row_count = query_rows.shape[0]
    block_rows = min(512, row_count)
    scale_factor = query_rows.shape[-1] ** (-0.5)
    grad_key = jnp.zeros(key_rows.shape, jnp.float32)
    grad_value = jnp.zeros(value_rows.shape, jnp.float32)
    scores = score_block(query_rows, key_rows, doc_rows, doc_rows)
    probs = jnp.exp(scores - log_sums)
    grad_probs = jnp.einsum(
        "qgrd,kgd->grqk", grad_att, value_rows, preferred_element_type=jnp.float32
    )
    inner = jnp.sum(probs * grad_probs, axis=-1, keepdims=True)
    grad_scores = (probs * (grad_probs - inner)).astype(jnp.bfloat16)
    query_parts = (
        jnp.einsum("grqk,kgd->qgrd", grad_scores, key_rows, preferred_element_type=jnp.float32)
        * scale_factor
    )
    grad_key = grad_key.at[:block_rows].add(
        jnp.einsum("grqk,qgrd->kgd", grad_scores, query_rows, preferred_element_type=jnp.float32)
        * scale_factor
    )
    grad_value = grad_value.at[:block_rows].add(
        jnp.einsum(
            "grqk,qgrd->kgd",
            probs.astype(jnp.bfloat16),
            grad_att,
            preferred_element_type=jnp.float32,
        )
    )
    return (query_parts, grad_key, grad_value)


def expert_forward(in_piece, down_piece, rows_here):
    both_parts = jnp.einsum("ecd,edf->ecf", rows_here, in_piece, preferred_element_type=jnp.float32)
    half_width = both_parts.shape[-1] // 2
    hidden = (jax.nn.silu(both_parts[..., :half_width]) * both_parts[..., half_width:]).astype(
        jnp.bfloat16
    )
    expert_out = jnp.einsum("ecf,efd->ecd", hidden, down_piece, preferred_element_type=jnp.float32)
    return (both_parts, hidden, expert_out)


def expert_backward(in_piece, down_piece, rows_here, both_parts, hidden, grad_out_here):
    half_width = both_parts.shape[-1] // 2
    gate_part, up_part = (both_parts[..., :half_width], both_parts[..., half_width:])
    grad_down = jnp.einsum(
        "ecf,ecd->efd", hidden, grad_out_here, preferred_element_type=jnp.float32
    )
    grad_hidden = jnp.einsum(
        "ecd,efd->ecf", grad_out_here, down_piece, preferred_element_type=jnp.float32
    )
    sigmoid_gate = jax.nn.sigmoid(gate_part)
    grad_gate = grad_hidden * up_part * sigmoid_gate * (1.0 + gate_part * (1.0 - sigmoid_gate))
    grad_up = grad_hidden * jax.nn.silu(gate_part)
    grad_both = jnp.concatenate([grad_gate, grad_up], axis=-1).astype(jnp.bfloat16)
    grad_in = jnp.einsum("ecd,ecf->edf", rows_here, grad_both, preferred_element_type=jnp.float32)
    grad_rows = jnp.einsum("ecf,edf->ecd", grad_both, in_piece, preferred_element_type=jnp.float32)
    return (grad_in, grad_down, grad_rows)


def shards(
    tokens,
    doc_ids,
    routes,
    norm_in_gain,
    w_query,
    w_key,
    w_value,
    w_out,
    norm_mid_gain,
    w_router,
    w_expert_in,
    w_expert_down,
    cotangent,
):
    row_count, model_width = tokens.shape
    groups = HEADS // KV_HEADS
    query_cols = w_query.shape[1]
    kv_cols = w_key.shape[1]
    inputs = tokens.astype(jnp.float32)
    grad_final = cotangent.astype(jnp.float32)
    cosine, sine_table = rotary_tables(positions(doc_ids), HEAD_DIM)
    normed_in, scale_in = normalize(inputs)
    gain_piece = lax.all_gather(norm_in_gain, "shard", axis=0, tiled=True)
    query_piece = lax.all_gather(w_query, "shard", axis=0, tiled=True)
    key_piece = lax.all_gather(w_key, "shard", axis=0, tiled=True)
    value_piece = lax.all_gather(w_value, "shard", axis=0, tiled=True)
    part_low = (normed_in * gain_piece.astype(jnp.float32)).astype(jnp.bfloat16)
    query_pre = jnp.dot(part_low, query_piece, preferred_element_type=jnp.float32)
    key_pre = jnp.dot(part_low, key_piece, preferred_element_type=jnp.float32)
    value_pre = jnp.dot(part_low, value_piece, preferred_element_type=jnp.float32)
    first_low = part_low
    gain_in_full = gain_piece
    query_rows = (
        rotate(query_pre.reshape(row_count, HEADS, HEAD_DIM), cosine, sine_table)
        .astype(jnp.bfloat16)
        .reshape(row_count, KV_HEADS, groups, HEAD_DIM)
    )
    key_rows = rotate(key_pre.reshape(row_count, KV_HEADS, HEAD_DIM), cosine, sine_table).astype(
        jnp.bfloat16
    )
    value_rows = value_pre.astype(jnp.bfloat16).reshape(row_count, KV_HEADS, HEAD_DIM)
    att_rows, log_sums = attend(query_rows, key_rows, value_rows, doc_ids)
    att_low = att_rows.reshape(row_count, query_cols)
    out_piece = lax.all_gather(w_out, "shard", axis=0, tiled=True)
    gain_piece = lax.all_gather(norm_mid_gain, "shard", axis=0, tiled=True)
    router_piece = lax.all_gather(w_router, "shard", axis=0, tiled=True)
    part_low = att_low
    branch_out = jnp.dot(part_low, out_piece, preferred_element_type=jnp.float32)
    middle = inputs + branch_out
    normed_mid, scale_mid = normalize(middle)
    second_low = (normed_mid * gain_piece.astype(jnp.float32)).astype(jnp.bfloat16)
    logits = jnp.dot(second_low, router_piece, preferred_element_type=jnp.float32)
    route_onehot = (
        routes[:, :, None] == jnp.arange(EXPERTS, dtype=jnp.int32)[None, None, :]
    ).astype(jnp.float32)
    chosen = jnp.sum(logits[:, None, :] * route_onehot, axis=-1)
    chosen_max = jnp.max(chosen, axis=1, keepdims=True)
    gate_exp = jnp.exp(chosen - chosen_max)
    gates = gate_exp / jnp.sum(gate_exp, axis=1, keepdims=True)
    token_of, route_of, filled = dispatch(routes)
    fill_mask = filled.astype(jnp.float32)
    slot_gates = gates.reshape(-1)[route_of] * fill_mask
    expert_rows = (second_low[token_of] * filled.astype(jnp.bfloat16)[:, None]).reshape(
        EXPERTS, CAP, model_width
    )
    grad_expert_out = (
        (grad_final[token_of] * slot_gates[:, None])
        .astype(jnp.bfloat16)
        .reshape(EXPERTS, CAP, model_width)
    )
    zero_rows = jnp.zeros((row_count, model_width), jnp.float32)
    in_piece = lax.all_gather(w_expert_in, "shard", axis=0, tiled=True)
    down_piece = lax.all_gather(w_expert_down, "shard", axis=0, tiled=True)
    both_parts, hidden, expert_out = expert_forward(in_piece, down_piece, expert_rows)
    out_flat = expert_out.reshape(-1, model_width)
    tokens_here = token_of
    added = out_flat * slot_gates[:, None]
    gate_grad_here = jnp.sum(out_flat * grad_final[tokens_here], axis=-1)
    combined = zero_rows.at[tokens_here].add(added)
    grad_in_here, grad_down_here, grad_rows_here = expert_backward(
        lax.all_gather(w_expert_in, "shard", axis=0, tiled=True),
        lax.all_gather(w_expert_down, "shard", axis=0, tiled=True),
        expert_rows,
        both_parts,
        hidden,
        grad_expert_out,
    )
    tokens_here = token_of
    grad_second = zero_rows.at[tokens_here].add(grad_rows_here.reshape(-1, model_width))
    grad_in_own, grad_down_own = (
        lax.psum_scatter(
            grad_in_here.astype(jnp.bfloat16), "shard", scatter_dimension=0, tiled=True
        ).astype(jnp.float32),
        lax.psum_scatter(
            grad_down_here.astype(jnp.bfloat16), "shard", scatter_dimension=0, tiled=True
        ).astype(jnp.float32),
    )
    mixed = (middle + combined).astype(jnp.bfloat16)
    grad_gates = (
        jnp.zeros((row_count * TOP_K,), jnp.float32)
        .at[route_of]
        .add(gate_grad_here * fill_mask)
        .reshape(row_count, TOP_K)
    )
    grad_chosen = gates * (grad_gates - jnp.sum(gates * grad_gates, axis=1, keepdims=True))
    grad_logits = jnp.sum(grad_chosen[:, :, None] * route_onehot, axis=1).astype(jnp.bfloat16)
    grad_router = jnp.einsum(
        "td,te->de", second_low, grad_logits, preferred_element_type=jnp.float32
    )
    grad_second = grad_second + jnp.einsum(
        "te,de->td", grad_logits, router_piece, preferred_element_type=jnp.float32
    )
    grad_mid_norm, grad_gain_mid = norm_back(
        grad_second, normed_mid, scale_mid, gain_piece.astype(jnp.float32)
    )
    grad_middle = grad_final + grad_mid_norm
    grad_branch = grad_middle.astype(jnp.bfloat16)
    grad_out_w = jnp.einsum("ta,td->ad", att_low, grad_branch, preferred_element_type=jnp.float32)
    grad_att = jnp.einsum(
        "td,ad->ta",
        grad_branch,
        lax.all_gather(w_out, "shard", axis=0, tiled=True),
        preferred_element_type=jnp.float32,
    ).astype(jnp.bfloat16)
    grad_query_rot, grad_key_rot, grad_value_rows = attend_back(
        query_rows,
        key_rows,
        value_rows,
        doc_ids,
        log_sums,
        grad_att.reshape(row_count, KV_HEADS, groups, HEAD_DIM),
    )
    grad_query_pre = (
        unrotate(grad_query_rot.reshape(row_count, HEADS, HEAD_DIM), cosine, sine_table)
        .astype(jnp.bfloat16)
        .reshape(row_count, query_cols)
    )
    grad_key_pre = (
        unrotate(grad_key_rot, cosine, sine_table).astype(jnp.bfloat16).reshape(row_count, kv_cols)
    )
    grad_value_pre = grad_value_rows.astype(jnp.bfloat16).reshape(row_count, kv_cols)
    grad_query_w = jnp.einsum(
        "td,tc->dc", first_low, grad_query_pre, preferred_element_type=jnp.float32
    )
    grad_key_w = jnp.einsum(
        "td,tc->dc", first_low, grad_key_pre, preferred_element_type=jnp.float32
    )
    grad_value_w = jnp.einsum(
        "td,tc->dc", first_low, grad_value_pre, preferred_element_type=jnp.float32
    )
    query_piece = lax.all_gather(w_query, "shard", axis=0, tiled=True)
    key_piece = lax.all_gather(w_key, "shard", axis=0, tiled=True)
    value_piece = lax.all_gather(w_value, "shard", axis=0, tiled=True)
    columns = jnp.einsum(
        "tc,dc->td", grad_query_pre, query_piece, preferred_element_type=jnp.float32
    )
    columns = columns + jnp.einsum(
        "tc,dc->td", grad_key_pre, key_piece, preferred_element_type=jnp.float32
    )
    columns = columns + jnp.einsum(
        "tc,dc->td", grad_value_pre, value_piece, preferred_element_type=jnp.float32
    )
    grad_in_norm, grad_gain_in = norm_back(
        columns, normed_in, scale_in, gain_in_full.astype(jnp.float32)
    )
    grad_tokens = grad_middle + grad_in_norm
    gain_in_own, query_own, key_own, value_own, out_own, gain_mid_own, router_own = (
        lax.psum_scatter(
            grad_gain_in.astype(jnp.bfloat16), "shard", scatter_dimension=0, tiled=True
        ).astype(jnp.float32),
        lax.psum_scatter(
            grad_query_w.astype(jnp.bfloat16), "shard", scatter_dimension=0, tiled=True
        ).astype(jnp.float32),
        lax.psum_scatter(
            grad_key_w.astype(jnp.bfloat16), "shard", scatter_dimension=0, tiled=True
        ).astype(jnp.float32),
        lax.psum_scatter(
            grad_value_w.astype(jnp.bfloat16), "shard", scatter_dimension=0, tiled=True
        ).astype(jnp.float32),
        lax.psum_scatter(
            grad_out_w.astype(jnp.bfloat16), "shard", scatter_dimension=0, tiled=True
        ).astype(jnp.float32),
        lax.psum_scatter(
            grad_gain_mid.astype(jnp.bfloat16), "shard", scatter_dimension=0, tiled=True
        ).astype(jnp.float32),
        lax.psum_scatter(
            grad_router.astype(jnp.bfloat16), "shard", scatter_dimension=0, tiled=True
        ).astype(jnp.float32),
    )
    (
        gain_in_own,
        query_own,
        key_own,
        value_own,
        out_own,
        gain_mid_own,
        router_own,
        grad_in_own,
        grad_down_own,
    ) = (
        lax.psum(gain_in_own.astype(jnp.bfloat16), "rep").astype(jnp.float32),
        lax.psum(query_own.astype(jnp.bfloat16), "rep").astype(jnp.float32),
        lax.psum(key_own.astype(jnp.bfloat16), "rep").astype(jnp.float32),
        lax.psum(value_own.astype(jnp.bfloat16), "rep").astype(jnp.float32),
        lax.psum(out_own.astype(jnp.bfloat16), "rep").astype(jnp.float32),
        lax.psum(gain_mid_own.astype(jnp.bfloat16), "rep").astype(jnp.float32),
        lax.psum(router_own.astype(jnp.bfloat16), "rep").astype(jnp.float32),
        lax.psum(grad_in_own.astype(jnp.bfloat16), "rep").astype(jnp.float32),
        lax.psum(grad_down_own.astype(jnp.bfloat16), "rep").astype(jnp.float32),
    )
    return (
        mixed,
        grad_tokens,
        gain_in_own,
        query_own,
        key_own,
        value_own,
        out_own,
        gain_mid_own,
        router_own,
        grad_in_own,
        grad_down_own,
    )


def solution(mesh):
    in_specs = (
        P(("rep", "shard"), None),
        P(("rep", "shard")),
        P(("rep", "shard"), None),
        P("shard"),
        P("shard", None),
        P("shard", None),
        P("shard", None),
        P("shard", None),
        P("shard"),
        P("shard", None),
        P("shard", None, None),
        P("shard", None, None),
        P(("rep", "shard"), None),
    )
    out_specs = (
        P(("rep", "shard"), None),
        P(("rep", "shard"), None),
        P("shard"),
        P("shard", None),
        P("shard", None),
        P("shard", None),
        P("shard", None),
        P("shard"),
        P("shard", None),
        P("shard", None, None),
        P("shard", None, None),
    )
    return jax.shard_map(shards, mesh=mesh, in_specs=in_specs, out_specs=out_specs, check_vma=False)
```

profile of v0, /device:TPU:0, one launch (start us, length us, event | category | flops | bytes accessed | tf_op | source)
XLA Modules:
  0.0 2448.3 jit_solution(8315457590984949947)
XLA Ops:
  11.7 12.7 all-gather
  38.7 15.5 scatter_custom_fusion
  55.3 15.1 gather_fusion.2
  70.4 13.2 all_gather.41
  89.2 27.4 %all-gather.13.cloned.1.call-done = bf16[1024,1024]{1,0:T(8,128)(2,1)} async-done(((bf16[256,1024]{1,0:T(8,128)(2,1)}), bf16[1024,1024]{1,0:T(8,128)(2,1)}) %all-gather.13.cloned.1.call-update) | async-done | bytes 2097168 | tf_op jit(solution)/shard_map/all_gather | solution.py:191
  143.8 18.8 all-gather.15.cloned.1.call-done
  167.1 15.0 gather_fusion
  183.3 540.9 %all-gather.17.cloned.1.call-done = bf16[16,1024,1024]{2,1,0:T(8,128)(2,1)} async-done(((bf16[4,1024,1024]{2,1,0:T(8,128)(2,1)}), bf16[16,1024,1024]{2,1,0:T(8,128)(2,1)}) %all-gather.17.cloned.1.call-update) | async-done | bytes 33554448 | tf_op jit(solution)/shard_map/all_gather | solution.py:239
  724.2 24.8 %fusion.11 = f32[16,288,1024]{2,1,0:T(8,128)} fusion(bf16[16,1024,1024]{2,1,0:T(8,128)(2,1)} %all-gather.17.cloned.1.call-done, bf16[16,288,1024]{2,1,0:T(8,128)(2,1)} %bitcast.127, bf16[16,288]{1,0:T(8,128)(2,1)S(1)} %reshape.387), kind=kOutput, calls=%fused_computation.33 | convolution fusion | flops 9668395008 | bytes 61875200 | tf_op jit(solution)/shard_map/ecd,edf->ecf/dot_general | solution.py:140
  749.0 10.4 multiply_convert_fusion.3
  759.3 251.3 %all-gather.19.cloned.1.call-done = bf16[16,512,1024]{2,1,0:T(8,128)(2,1)} async-done(((bf16[4,512,1024]{2,1,0:T(8,128)(2,1)}), bf16[16,512,1024]{2,1,0:T(8,128)(2,1)}) %all-gather.19.cloned.1.call-update) | async-done | bytes 16777232 | tf_op jit(solution)/shard_map/all_gather | solution.py:240
  1010.6 19.9 multiply_reduce_fusion
  1030.6 32.1 %scatter_custom_fusion.2 = f32[4096]{0:T(1024)S(1)} fusion(s32[4608]{0:T(1024)S(1)} %get-tuple-element.68, f32[4608]{0:T(1024)S(1)} %broadcast_select_fusion, f32[]{:T(128)} %constant.122.clone.1), kind=kCustom, calls=%fused_computation.129 | custom fusion | flops 4608 | bytes 16388 | tf_op jit(solution)/shard_map/scatter-add | solution.py:269
  1063.2 24.5 %gather_fusion.1 = f32[4608]{0:T(1024)S(1)} fusion(f32[4096]{0:T(1024)S(1)} %div.73, s32[5120]{0:T(1024)S(1)} %pad_clamp_fusion), kind=kCustom, calls=%fused_computation.1 | custom fusion | bytes 55296 | tf_op jit(solution)/shard_map/gather | solution.py:229
  1089.7 25.8 %multiply_convert_fusion.2 = (bf16[16,288,512]{2,1,0:T(8,128)(2,1)}, bf16[16,288,512]{2,1,0:T(8,128)(2,1)}) fusion(f32[16,288,1024]{2,1,0:T(8,128)} %fusion.11, bf16[16,512,1024]{2,1,0:T(8,128)(2,1)} %all-gather.19.cloned.1.call-done, f32[16,288,1024]{2,1,0:T(8,128)} %bitcast.124, f32[16,288]{1,0:T(8,128)S(1)} %mul.406), kind=kOutput, calls=%fused_computation.25 | convolution fusion | flops 4871946240 | bytes 63981568 | tf_op jit(solution)/shard_map/ecd,efd->ecf/dot_general | solution.py:155
  1115.5 23.2 fusion.13
  1138.7 43.6 %scatter_fusion.1 = f32[512,1024]{1,0:T(8,128)} fusion(f32[512,1024]{1,0:T(8,128)} %fusion.74, s32[4608]{0:T(1024)S(1)} %copy-done.40, f32[4608,1024]{1,0:T(8,128)} %bitcast.126), kind=kCustom, calls=%fused_computation.6 | custom fusion | flops 4718592 | bytes 56641536 | tf_op jit(solution)/shard_map/scatter-add | solution.py:256
  1190.7 11.4 fusion
  1202.1 12.3 fusion.2
  1220.9 9.0 fusion.34
  1246.9 18.4 convolution_convert_fusion.1
  1266.0 27.6 %convolution_convert_fusion = bf16[16,1024,1024]{2,1,0:T(8,128)(2,1)} fusion(bf16[16,288,1024]{2,1,0:T(8,128)(2,1)} %bitcast.128, bf16[16,288,512]{2,1,0:T(8,128)(2,1)} %get-tuple-element.71, bf16[16,288,512]{2,1,0:T(8,128)(2,1)} %get-tuple-element.70, bf16[16,288]{1,0:T(8,128)(2,1)S(1)} %copy-done.61), kind=kOutput, calls=%fused_computation.7 | convolution fusion | flops 9704046592 | bytes 52438016 | tf_op jit(solution)/shard_map/ecd,ecf->edf/dot_general | solution.py:162
  1295.8 24.2 reduce-scatter.8.cloned.1.call-done
  1320.0 45.5 %reduce-scatter.14.cloned.1.call-done = bf16[256,1024]{1,0:T(8,128)(2,1)} async-done(((bf16[1024,1024]{1,0:T(8,128)(2,1)}), bf16[256,1024]{1,0:T(8,128)(2,1)}) %reduce-scatter.14.cloned.1.call-update) | async-done | bytes 524304 | tf_op jit(solution)/shard_map/reduce_scatter | solution.py:347
  1365.4 282.6 %reduce-scatter.20.cloned.1.call-done = bf16[4,512,1024]{2,1,0:T(8,128)(2,1)} async-done(((bf16[16,512,1024]{2,1,0:T(8,128)(2,1)}), bf16[4,512,1024]{2,1,0:T(8,128)(2,1)}) %reduce-scatter.20.cloned.1.call-update) | async-done | bytes 4194320 | tf_op jit(solution)/shard_map/reduce_scatter | solution.py:261
  1648.1 555.1 %reduce-scatter.18.cloned.1.call-done = bf16[4,1024,1024]{2,1,0:T(8,128)(2,1)} async-done(((bf16[16,1024,1024]{2,1,0:T(8,128)(2,1)}), bf16[4,1024,1024]{2,1,0:T(8,128)(2,1)}) %reduce-scatter.18.cloned.1.call-update) | async-done | bytes 8388624 | tf_op jit(solution)/shard_map/reduce_scatter | solution.py:258
  2213.1 11.4 all-reduce.4
  2224.7 15.2 bitcast_multiply_fusion
  2239.9 41.5 %scatter_fusion = f32[512,1024]{1,0:T(8,128)S(1)} fusion(f32[512,1024]{1,0:T(8,128)S(1)} %copy-done.1, s32[4608]{0:T(1024)S(1)} %copy-done.41, f32[4608,1024]{1,0:T(8,128)} %bitcast_multiply_fusion), kind=kCustom, calls=%fused_computation.4 | custom fusion | flops 4718592 | bytes 56641536 | tf_op jit(solution)/shard_map/scatter-add | solution.py:246
  2286.8 13.3 all-reduce.2
  2301.8 119.3 %all-reduce.7.cloned.1.call-done = (bf16[256,1024]{1,0:T(8,128)(2,1)}, bf16[256,512]{1,0:T(8,128)(2,1)}, bf16[256,512]{1,0:T(8,128)(2,1)}, bf16[256,1024]{1,0:T(...) async-done(((bf16[256,1024]{1,0:T(8,128)(2,1)}, bf16[256,512]{1,0:T(8,128)(2,1)}, bf16[256,512]{1,0:T(8,128)(2,1)}, bf16[256,1024]{1,0:T(8,128)(2,1)}, ...) | async-done | bytes 14155792 | tf_op jit(solution)/shard_map/psum | solution.py:369
  2421.1 11.9 convert_element_type.208
  (264 shorter events, 119.3 us)
Async XLA Ops:
  7.2 77.5 %all-gather.11.cloned.1.call-start = ((), (), s32[]{:S(2)}) async-start(), calls=%async_computation.8 | async-start | bytes 1310720 | tf_op jit(solution)/shard_map/all_gather | solution.py:192
  7.9 79.0 %all-gather.9.cloned.1.call-start = ((), (), s32[]{:S(2)}) async-start(), calls=%async_computation.7 | async-start | bytes 1310720 | tf_op jit(solution)/shard_map/all_gather | solution.py:193
  8.7 107.9 %all-gather.13.cloned.1.call-start = ((), (), s32[]{:S(2)}) async-start(), calls=%async_computation.9 | async-start | bytes 2621440 | tf_op jit(solution)/shard_map/all_gather | solution.py:191
  9.4 153.2 %all-gather.15.cloned.1.call-start = ((), (), s32[]{:S(2)}) async-start(), calls=%async_computation.10 | async-start | bytes 2621440 | tf_op jit(solution)/shard_map/all_gather | solution.py:211
  10.0 714.2 %all-gather.17.cloned.1.call-start = ((), (), s32[]{:S(2)}) async-start(), calls=%async_computation.11 | async-start | bytes 41943040 | tf_op jit(solution)/shard_map/all_gather | solution.py:239
  10.6 43.7 %copy-start.12 = (bf16[512,1024]{1,0:T(8,128)(2,1)S(1)}, bf16[512,1024]{1,0:T(8,128)(2,1)}, u32[]{:S(2)}) copy-start(bf16[512,1024]{1,0:T(8,128)(2,1)} %param.33) | copy-start | bytes 3145732
  10.6 1000.0 %all-gather.19.cloned.1.call-start = ((), (), s32[]{:S(2)}) async-start(), calls=%async_computation.12 | async-start | bytes 20971520 | tf_op jit(solution)/shard_map/all_gather | solution.py:240
  11.2 1284.6 %reduce-scatter.10.cloned.1.call-start = ((), (), s32[]{:S(2)}) async-start(), calls=%async_computation.14 | async-start | bytes 1310720 | tf_op jit(solution)/shard_map/reduce_scatter | solution.py:341
  24.4 92.2 %copy-start.53 = (f32[4,1,256]{2,1,0:T(1,128)}, f32[4,1,256]{2,1,0:T(1,128)S(1)}, u32[]{:S(2)}) copy-start(f32[4,1,256]{2,1,0:T(1,128)S(1)} %convert_element_type.211) | copy-start | bytes 12292
  32.7 132.9 %copy-start.51 = (f32[4,1,256]{2,1,0:T(1,128)}, f32[4,1,256]{2,1,0:T(1,128)S(1)}, u32[]{:S(2)}) copy-start(f32[4,1,256]{2,1,0:T(1,128)S(1)} %convert_element_type.212) | copy-start | bytes 12292
  54.3 669.8 %copy-start.60 = (bf16[16,288]{1,0:T(8,128)(2,1)}, bf16[16,288]{1,0:T(8,128)(2,1)S(1)}, u32[]{:S(2)}) copy-start(bf16[16,288]{1,0:T(8,128)(2,1)S(1)} %reshape.387) | copy-start | bytes 27652
  55.2 28.5 %copy-start.6 = (bf16[512,1024]{1,0:T(8,128)(2,1)S(1)}, bf16[512,1024]{1,0:T(8,128)(2,1)}, u32[]{:S(2)}) copy-start(bf16[512,1024]{1,0:T(8,128)(2,1)} %param.21) | copy-start | bytes 3145732
  84.0 32.6 %copy-start.58 = (f32[512]{0:T(512)}, f32[512]{0:T(512)S(1)}, u32[]{:S(2)}) copy-start(f32[512]{0:T(512)S(1)} %add_rsqrt_fusion.1) | copy-start | bytes 6148
  84.4 35.2 %copy-start.23 = (f32[512,32]{0,1:T(8,128)}, f32[512,32]{0,1:T(8,128)S(1)}, u32[]{:S(2)}) copy-start(f32[512,32]{0,1:T(8,128)S(1)} %get-tuple-element.80) | copy-start | bytes 196612
  84.4 35.2 %copy-start.25 = (f32[512,32]{0,1:T(8,128)}, f32[512,32]{0,1:T(8,128)S(1)}, u32[]{:S(2)}) copy-start(f32[512,32]{0,1:T(8,128)S(1)} %get-tuple-element.81) | copy-start | bytes 196612
  86.9 33.1 %copy-start.28 = (bf16[512,8,32]{0,2,1:T(8,128)(2,1)}, bf16[512,8,32]{0,2,1:T(8,128)(2,1)S(1)}, u32[]{:S(2)}) copy-start(bf16[512,8,32]{0,2,1:T(8,128)(2,1)S(1)} %get-tuple-element.78) | copy-start | bytes 786436
  86.9 33.1 %copy-start.30 = (bf16[512,8,32]{0,2,1:T(8,128)(2,1)}, bf16[512,8,32]{0,2,1:T(8,128)(2,1)S(1)}, u32[]{:S(2)}) copy-start(bf16[512,8,32]{0,2,1:T(8,128)(2,1)S(1)} %get-tuple-element.79) | copy-start | bytes 786436
  89.2 47.0 %copy-start.33 = (bf16[512,512]{0,1:T(8,128)(2,1)}, bf16[512,512]{0,1:T(8,128)(2,1)S(1)}, u32[]{:S(2)}) copy-start(bf16[512,512]{0,1:T(8,128)(2,1)S(1)} %convolution_convert_fusion.7) | copy-start | bytes 1572868
  1087.8 27.7 %copy-start.45 = (f32[4608]{0:T(1024)}, f32[4608]{0:T(1024)S(1)}, u32[]{:S(2)}) copy-start(f32[4608]{0:T(1024)S(1)} %broadcast_select_fusion.1) | copy-start | bytes 55300
  1087.9 27.6 %copy-start.37 = (f32[16,288]{1,0:T(8,128)}, f32[16,288]{1,0:T(8,128)S(1)}, u32[]{:S(2)}) copy-start(f32[16,288]{1,0:T(8,128)S(1)} %mul.406) | copy-start | bytes 55300
  1087.9 27.5 %copy-start.47 = (bf16[512,16]{0,1:T(8,128)(2,1)}, bf16[512,16]{0,1:T(8,128)(2,1)S(1)}, u32[]{:S(2)}) copy-start(bf16[512,16]{0,1:T(8,128)(2,1)S(1)} %select_reduce_fusion) | copy-start | bytes 49156
  1115.5 23.2 copy-start.40
  1138.7 43.7 %copy-start.1 = (f32[512,1024]{1,0:T(8,128)S(1)}, f32[512,1024]{1,0:T(8,128)}, u32[]{:S(2)}) copy-start(f32[512,1024]{1,0:T(8,128)} %copy-done) | copy-start | bytes 6291460
  1138.7 43.7 %copy-start.52 = (f32[4,1,256]{2,1,0:T(1,128)S(1)}, f32[4,1,256]{2,1,0:T(1,128)}, u32[]{:S(2)}) copy-start(f32[4,1,256]{2,1,0:T(1,128)} %copy-done.51) | copy-start | bytes 12292
  1138.7 43.6 %copy-start.57 = (f32[512]{0:T(512)S(1)}, f32[512]{0:T(512)}, u32[]{:S(2)}) copy-start(f32[512]{0:T(512)} %copy-done.56) | copy-start | bytes 6148
  1220.8 75.0 %reduce-scatter.12.cloned.1.call-start = ((), (), s32[]{:S(2)}) async-start(), calls=%async_computation.15 | async-start | bytes 1310720 | tf_op jit(solution)/shard_map/reduce_scatter | solution.py:344
  1232.6 87.4 %reduce-scatter.8.cloned.1.call-start = ((), (), s32[]{:S(2)}) async-start(), calls=%async_computation.13 | async-start | bytes 2621440 | tf_op jit(solution)/shard_map/reduce_scatter | solution.py:338
  1242.0 123.5 %reduce-scatter.14.cloned.1.call-start = ((), (), s32[]{:S(2)}) async-start(), calls=%async_computation.16 | async-start | bytes 2621440 | tf_op jit(solution)/shard_map/reduce_scatter | solution.py:347
  1246.8 401.3 %reduce-scatter.20.cloned.1.call-start = ((), (), s32[]{:S(2)}) async-start(), calls=%async_computation.19 | async-start | bytes 20971520 | tf_op jit(solution)/shard_map/reduce_scatter | solution.py:261
  1265.3 937.9 %reduce-scatter.18.cloned.1.call-start = ((), (), s32[]{:S(2)}) async-start(), calls=%async_computation.18 | async-start | bytes 41943040 | tf_op jit(solution)/shard_map/reduce_scatter | solution.py:258
  1293.6 993.2 %reduce-scatter.16.cloned.1.call-start = ((), (), s32[]{:S(2)}) async-start(), calls=%async_computation.17 | async-start | bytes 40960 | tf_op jit(solution)/shard_map/reduce_scatter | solution.py:353
  1295.7 1125.4 %all-reduce.7.cloned.1.call-start = ((), (), s32[]{:S(2)}) async-start(), calls=%async_computation.20 | async-start | bytes 28311552 | tf_op jit(solution)/shard_map/psum | solution.py:369
  (48 other events, 317.8 us)
Sparse Core Ops, SparseCore 0:
  9.6 30.7 all-gather.10
  41.9 27.3 all-gather.8
  70.9 45.6 all-gather.12
  118.0 44.5 all-gather.14
  164.0 560.1 all-gather.16
  725.6 284.9 all-gather.18
  1221.0 25.3 reduce-scatter.9
  1248.7 25.7 reduce-scatter.11
  1277.4 42.5 reduce-scatter.7
  1322.2 43.1 reduce-scatter.13
  1368.4 279.6 reduce-scatter.19
  1650.4 552.7 reduce-scatter.17
  2206.0 19.6 reduce-scatter.15
  2230.9 190.1 all-reduce.6
where the time goes:
time: 2460 us; the launch traced here: 2450 us
  waiting for transfers between devices  1870 us (76%)
  matrix products  218 us (9%)
  other arithmetic  203 us (8%)
  local copies, waits for them, and re-layouts  83.9 us (3%)
  blocking collectives  58.2 us (2%)
    reduce_scatter x1, waiting for transfers between devices, shards(): lax.psum_scatter(grad_in_here.astype(jnp.bfloat16), 'shard', scatter_dime...  555 us
    all_gather x1, waiting for transfers between devices, shards(): in_piece = lax.all_gather(w_expert_in, 'shard', axis=0, tiled=True)  541 us
    reduce_scatter x1, waiting for transfers between devices, shards(): lax.psum_scatter(grad_down_here.astype(jnp.bfloat16), 'shard', scatter_di...  283 us
    all_gather x1, waiting for transfers between devices, shards(): down_piece = lax.all_gather(w_expert_down, 'shard', axis=0, tiled=True)  251 us
    psum x1, waiting for transfers between devices, shards(): lax.psum(query_own.astype(jnp.bfloat16), 'rep').astype(jnp.float32)  119 us
  transfers between devices with their start and end apart: 14, of which 9 were waited for; matrix products, arithmetic and copies ran while one was open for 11% of the time, Pallas kernels for 0%

commit v1 on v0

v1 whole, which is shorter than its diff:
```python
import jax
import jax.numpy as jnp
from jax import lax
from jax.sharding import PartitionSpec as P

HEADS = 16
KV_HEADS = 8
HEAD_DIM = 64
EXPERTS = 16
PAD = 128


epsilon = 1e-06
rope_base = 10000.0
masked_score = -1e30


def positions(doc_rows):
    row_count = doc_rows.shape[0]
    places = jnp.arange(row_count, dtype=jnp.int32)
    opening = jnp.concatenate([jnp.ones((1,), dtype=jnp.bool_), doc_rows[1:] != doc_rows[:-1]])
    begins = lax.cummax(jnp.where(opening, places, 0), axis=0)
    return places - begins


def rotary_tables(places, head_width):
    half_width = head_width // 2
    frequencies = jnp.power(
        rope_base, -2.0 * jnp.arange(half_width, dtype=jnp.float32) / head_width
    )
    angles = places.astype(jnp.float32)[:, None] * frequencies[None, :]
    return (jnp.cos(angles)[:, None, :], jnp.sin(angles)[:, None, :])


def rotate(values, cosine, sine_table):
    half_width = values.shape[-1] // 2
    former, latter = (values[..., :half_width], values[..., half_width:])
    return jnp.concatenate(
        [former * cosine - latter * sine_table, latter * cosine + former * sine_table], axis=-1
    )


def unrotate(values, cosine, sine_table):
    half_width = values.shape[-1] // 2
    former, latter = (values[..., :half_width], values[..., half_width:])
    return jnp.concatenate(
        [former * cosine + latter * sine_table, latter * cosine - former * sine_table], axis=-1
    )


def normalize(values):
    row_scale = lax.rsqrt(jnp.mean(values * values, axis=-1, keepdims=True) + epsilon)
    return (values * row_scale, row_scale)


def norm_back(grad_scaled, normed, row_scale, gain_full):
    grad_normed = grad_scaled * gain_full
    inner = jnp.mean(grad_normed * normed, axis=-1, keepdims=True)
    return (row_scale * (grad_normed - normed * inner), jnp.sum(grad_scaled * normed, axis=0))


def score_block(query_blk, key_part, doc_query, doc_key):
    scores = jnp.einsum(
        "qgrd,kgd->grqk", query_blk, key_part, preferred_element_type=jnp.float32
    ) * query_blk.shape[-1] ** (-0.5)
    query_place = jnp.arange(query_blk.shape[0], dtype=jnp.int32)
    key_place = jnp.arange(key_part.shape[0], dtype=jnp.int32)
    allowed = (doc_query[:, None] == doc_key[None, :]) & (
        query_place[:, None] >= key_place[None, :]
    )
    return jnp.where(allowed, scores, masked_score)


def attend(query_rows, key_rows, value_rows, doc_rows):
    scores = score_block(query_rows, key_rows, doc_rows, doc_rows)
    row_max = jnp.max(scores, axis=-1, keepdims=True)
    exponent = jnp.exp(scores - row_max)
    row_total = jnp.sum(exponent, axis=-1, keepdims=True)
    probs_low = (exponent / row_total).astype(jnp.bfloat16)
    outputs = jnp.einsum(
        "grqk,kgd->qgrd", probs_low, value_rows, preferred_element_type=jnp.float32
    ).astype(jnp.bfloat16)
    lse_parts = row_max + jnp.log(row_total)
    return (outputs, lse_parts)


def attend_back(query_rows, key_rows, value_rows, doc_rows, log_sums, grad_att):
    row_count = query_rows.shape[0]
    block_rows = min(512, row_count)
    scale_factor = query_rows.shape[-1] ** (-0.5)
    grad_key = jnp.zeros(key_rows.shape, jnp.float32)
    grad_value = jnp.zeros(value_rows.shape, jnp.float32)
    scores = score_block(query_rows, key_rows, doc_rows, doc_rows)
    probs = jnp.exp(scores - log_sums)
    grad_probs = jnp.einsum(
        "qgrd,kgd->grqk", grad_att, value_rows, preferred_element_type=jnp.float32
    )
    inner = jnp.sum(probs * grad_probs, axis=-1, keepdims=True)
    grad_scores = (probs * (grad_probs - inner)).astype(jnp.bfloat16)
    query_parts = (
        jnp.einsum("grqk,kgd->qgrd", grad_scores, key_rows, preferred_element_type=jnp.float32)
        * scale_factor
    )
    grad_key = grad_key.at[:block_rows].add(
        jnp.einsum("grqk,qgrd->kgd", grad_scores, query_rows, preferred_element_type=jnp.float32)
        * scale_factor
    )
    grad_value = grad_value.at[:block_rows].add(
        jnp.einsum(
            "grqk,qgrd->kgd",
            probs.astype(jnp.bfloat16),
            grad_att,
            preferred_element_type=jnp.float32,
        )
    )
    return (query_parts, grad_key, grad_value)


def gather_shard(piece):
    return lax.all_gather(piece, "shard", axis=0, tiled=True)


def shards(
    tokens,
    doc_ids,
    routes,
    norm_in_gain,
    w_query,
    w_key,
    w_value,
    w_out,
    norm_mid_gain,
    w_router,
    w_expert_in,
    w_expert_down,
    cotangent,
):
    bf16, f32 = jnp.bfloat16, jnp.float32
    row_count, model_width = tokens.shape
    groups = HEADS // KV_HEADS
    query_cols = w_query.shape[1]
    kv_cols = w_key.shape[1]
    own_rows = w_query.shape[0]
    own_experts, ff = w_expert_down.shape[:2]
    shard_at = lax.axis_index("shard")

    small = jnp.concatenate(
        [
            w_router,
            norm_in_gain[:, None],
            norm_mid_gain[:, None],
            jnp.zeros((own_rows, PAD - EXPERTS - 2), bf16),
        ],
        axis=1,
    )
    qkv_full = gather_shard(jnp.concatenate([w_query, w_key, w_value, small], axis=1))
    qkv_w = qkv_full[:, : query_cols + 2 * kv_cols]
    small_full = qkv_full[:, query_cols + 2 * kv_cols :]
    router_full = small_full[:, :EXPERTS]
    gain_in = small_full[:, EXPERTS].astype(f32)
    gain_mid = small_full[:, EXPERTS + 1].astype(f32)
    out_w = gather_shard(w_out)
    mask_own = jnp.any(
        routes[:, :, None] == jnp.arange(EXPERTS, dtype=jnp.int32)[None, None, :], axis=1
    )
    side = jnp.concatenate(
        [cotangent, mask_own.astype(bf16), jnp.zeros((row_count, PAD - EXPERTS), bf16)], axis=1
    )
    side_all = gather_shard(side)
    dy_all = side_all[:, :model_width]
    mask_all = side_all[:, model_width : model_width + EXPERTS] > 0

    inputs = tokens.astype(f32)
    grad_final = cotangent.astype(f32)
    cosine, sine_table = rotary_tables(positions(doc_ids), HEAD_DIM)
    normed_in, scale_in = normalize(inputs)
    first_low = (normed_in * gain_in).astype(bf16)
    qkv_pre = jnp.dot(first_low, qkv_w, preferred_element_type=f32)
    query_pre = qkv_pre[:, :query_cols]
    key_pre = qkv_pre[:, query_cols : query_cols + kv_cols]
    value_pre = qkv_pre[:, query_cols + kv_cols :]
    query_rows = (
        rotate(query_pre.reshape(row_count, HEADS, HEAD_DIM), cosine, sine_table)
        .astype(bf16)
        .reshape(row_count, KV_HEADS, groups, HEAD_DIM)
    )
    key_rows = rotate(key_pre.reshape(row_count, KV_HEADS, HEAD_DIM), cosine, sine_table).astype(
        bf16
    )
    value_rows = value_pre.astype(bf16).reshape(row_count, KV_HEADS, HEAD_DIM)
    att_rows, log_sums = attend(query_rows, key_rows, value_rows, doc_ids)
    att_low = att_rows.reshape(row_count, query_cols)
    middle = inputs + jnp.dot(att_low, out_w, preferred_element_type=f32)
    normed_mid, scale_mid = normalize(middle)
    second_low = (normed_mid * gain_mid).astype(bf16)

    second_all = gather_shard(second_low)
    logits = jnp.dot(second_all, router_full, preferred_element_type=f32)
    chosen = jnp.where(mask_all, logits, masked_score)
    gate_exp = jnp.where(mask_all, jnp.exp(chosen - jnp.max(chosen, axis=1, keepdims=True)), 0.0)
    gates_all = gate_exp / jnp.sum(gate_exp, axis=1, keepdims=True)
    gates_here = lax.dynamic_slice_in_dim(gates_all, shard_at * own_experts, own_experts, axis=1)
    gates_own = lax.dynamic_slice_in_dim(gates_all, shard_at * row_count, row_count, axis=0)

    gated, grad_both, grad_gates_here = experts(
        second_all, dy_all, gates_here, w_expert_in, w_expert_down
    )
    combined = jnp.einsum("etf,efd->td", gated, w_expert_down, preferred_element_type=f32)
    combined_own = lax.psum_scatter(
        combined.astype(bf16), "shard", scatter_dimension=0, tiled=True
    )
    grad_second_here = jnp.einsum("etf,edf->td", grad_both, w_expert_in, preferred_element_type=f32)
    gate_cols = lax.dynamic_update_slice_in_dim(
        jnp.zeros((grad_gates_here.shape[0], EXPERTS), f32),
        grad_gates_here,
        shard_at * own_experts,
        axis=1,
    )
    gate_high = gate_cols.astype(bf16)
    gate_low = (gate_cols - gate_high.astype(f32)).astype(bf16)
    back_rows = jnp.concatenate(
        [
            grad_second_here.astype(bf16),
            gate_high,
            gate_low,
            jnp.zeros((gate_cols.shape[0], PAD - 2 * EXPERTS), bf16),
        ],
        axis=1,
    )
    back_own = lax.psum_scatter(back_rows, "shard", scatter_dimension=0, tiled=True)
    grad_in_here = jnp.einsum("td,etf->edf", second_all, grad_both, preferred_element_type=f32)
    grad_down_here = jnp.einsum("etf,td->efd", gated, dy_all, preferred_element_type=f32)
    grad_in_own = lax.psum(grad_in_here.astype(bf16), "rep").astype(f32)
    grad_down_own = lax.psum(grad_down_here.astype(bf16), "rep").astype(f32)

    mixed = (middle + combined_own.astype(f32)).astype(bf16)
    gate_back = back_own[:, model_width : model_width + 2 * EXPERTS].astype(f32)
    grad_gates = gate_back[:, :EXPERTS] + gate_back[:, EXPERTS:]
    grad_logits = (
        gates_own * (grad_gates - jnp.sum(gates_own * grad_gates, axis=1, keepdims=True))
    ).astype(bf16)
    grad_router = jnp.einsum("td,te->de", second_low, grad_logits, preferred_element_type=f32)
    grad_second = back_own[:, :model_width].astype(f32) + jnp.einsum(
        "te,de->td", grad_logits, router_full, preferred_element_type=f32
    )
    grad_mid_norm, grad_gain_mid = norm_back(grad_second, normed_mid, scale_mid, gain_mid)
    grad_middle = grad_final + grad_mid_norm
    grad_branch = grad_middle.astype(bf16)
    grad_out_w = jnp.einsum("ta,td->ad", att_low, grad_branch, preferred_element_type=f32)
    grad_att = jnp.einsum("td,ad->ta", grad_branch, out_w, preferred_element_type=f32).astype(bf16)
    grad_query_rot, grad_key_rot, grad_value_rows = attend_back(
        query_rows,
        key_rows,
        value_rows,
        doc_ids,
        log_sums,
        grad_att.reshape(row_count, KV_HEADS, groups, HEAD_DIM),
    )
    grad_query_pre = (
        unrotate(grad_query_rot.reshape(row_count, HEADS, HEAD_DIM), cosine, sine_table)
        .astype(bf16)
        .reshape(row_count, query_cols)
    )
    grad_key_pre = unrotate(grad_key_rot, cosine, sine_table).astype(bf16)
    grad_pre = jnp.concatenate(
        [
            grad_query_pre,
            grad_key_pre.reshape(row_count, kv_cols),
            grad_value_rows.astype(bf16).reshape(row_count, kv_cols),
        ],
        axis=1,
    )
    grad_qkv = jnp.einsum("td,tc->dc", first_low, grad_pre, preferred_element_type=f32)
    columns = jnp.einsum("tc,dc->td", grad_pre, qkv_w, preferred_element_type=f32)
    grad_in_norm, grad_gain_in = norm_back(columns, normed_in, scale_in, gain_in)
    grad_tokens = grad_middle + grad_in_norm

    joint = jnp.concatenate(
        [
            grad_qkv.astype(bf16),
            grad_out_w.astype(bf16),
            grad_router.astype(bf16),
            grad_gain_in.astype(bf16)[:, None],
            grad_gain_mid.astype(bf16)[:, None],
            jnp.zeros((model_width, PAD - EXPERTS - 2), bf16),
        ],
        axis=1,
    )
    joint_own = reduce_joint(joint).astype(f32)
    edges = [0]
    for width in (query_cols, kv_cols, kv_cols, w_out.shape[1], EXPERTS, 1, 1):
        edges.append(edges[-1] + width)
    pieces = [joint_own[:, a:b] for a, b in zip(edges[:-1], edges[1:])]
    query_own, key_own, value_own, out_own, router_own, gain_in_own, gain_mid_own = pieces
    return (
        mixed,
        grad_tokens,
        gain_in_own[:, 0],
        query_own,
        key_own,
        value_own,
        out_own,
        gain_mid_own[:, 0],
        router_own,
        grad_in_own,
        grad_down_own,
    )


def reduce_joint(joint):
    part = lax.psum_scatter(joint, "shard", scatter_dimension=0, tiled=True)
    return lax.psum(part, "rep")


def experts(rows, dy_rows, gates, in_w, down_w):
    f32, bf16 = jnp.float32, jnp.bfloat16
    both = jnp.einsum("td,edf->etf", rows, in_w, preferred_element_type=f32)
    half_width = both.shape[-1] // 2
    gate_part, up_part = (both[..., :half_width], both[..., half_width:])
    sigmoid_gate = jax.nn.sigmoid(gate_part)
    silu_gate = gate_part * sigmoid_gate
    hidden = (silu_gate * up_part).astype(bf16).astype(f32)
    back = jnp.einsum("td,efd->etf", dy_rows, down_w, preferred_element_type=f32)
    gate_cols = gates.T[:, :, None]
    grad_gates = jnp.sum(hidden * back, axis=-1).T
    gated = (hidden * gate_cols).astype(bf16)
    grad_hidden = back * gate_cols
    grad_gate = grad_hidden * up_part * sigmoid_gate * (1.0 + gate_part * (1.0 - sigmoid_gate))
    grad_both = jnp.concatenate([grad_gate, grad_hidden * silu_gate], axis=-1).astype(bf16)
    return (gated, grad_both, grad_gates)


def solution(mesh):
    in_specs = (
        P(("rep", "shard"), None),
        P(("rep", "shard")),
        P(("rep", "shard"), None),
        P("shard"),
        P("shard", None),
        P("shard", None),
        P("shard", None),
        P("shard", None),
        P("shard"),
        P("shard", None),
        P("shard", None, None),
        P("shard", None, None),
        P(("rep", "shard"), None),
    )
    out_specs = (
        P(("rep", "shard"), None),
        P(("rep", "shard"), None),
        P("shard"),
        P("shard", None),
        P("shard", None),
        P("shard", None),
        P("shard", None),
        P("shard"),
        P("shard", None),
        P("shard", None, None),
        P("shard", None, None),
    )
    return jax.shard_map(shards, mesh=mesh, in_specs=in_specs, out_specs=out_specs, check_vma=False)
```

time: 2460 us -> 1000 us (0.41)
  waiting for transfers between devices: 1870 us -> 663 us
  other arithmetic: 203 us -> 49.2 us
  blocking collectives: 58.2 us -> 0 us
    reduce_scatter x7 -> x3, waiting for transfers between devices: 907 us -> 220 us  [the longest x1 76.3 us: reduce_joint(): part = lax.psum_scatter(joint, 'shard', scatter_dimension=0, tiled=True)]
    all_gather x6 -> x4, waiting for transfers between devices: 838 us -> 251 us  [gather_shard(): return lax.all_gather(piece, 'shard', axis=0, tiled=True)]
    scatter-add x3 -> x0, other arithmetic: 117 us -> none  [the longest x1 43.6 us: shards(): zero_rows.at[tokens_here].add(grad_rows_here.reshape(-1, model_width))]
    psum x1, waiting for transfers between devices: 119 us -> 191 us  [shards(): grad_in_own = lax.psum(grad_in_here.astype(bf16), 'rep').astype(f32)]
    gather x3 -> x0, local copies, waits for them, and re-layouts: 54.7 us -> none  [the longest x1 24.5 us: shards(): slot_gates = gates.reshape(-1)[route_of] * fill_mask]
    all_gather x3 -> x0, blocking collectives: 33.6 us -> none  [the longest x1 13.2 us: shards(): router_piece = lax.all_gather(w_router, 'shard', axis=0, tiled=True)]
    dot_general x21 -> x15, matrix products: 174 us -> 158 us  [the longest x1 28.4 us: experts(): jnp.einsum('td,efd->etf', dy_rows, down_w, preferred_element_type=f32)]
  transfers between devices with their start and end apart: 14 -> 8, of which waited for: 9 -> 8; matrix products, arithmetic and copies ran while one was open for 11% -> 12% of each run, Pallas kernels for 0% -> 0%
where the time goes in v1:
time: 1000 us; the launch traced here: 990 us
  waiting for transfers between devices  663 us (66%)
  matrix products  202 us (20%)
  local copies, waits for them, and re-layouts  60.7 us (6%)
  other arithmetic  49.2 us (5%)
  between operations  15.4 us (2%)
    all_gather x4, waiting for transfers between devices, gather_shard(): return lax.all_gather(piece, 'shard', axis=0, tiled=True)  251 us
    psum x1, waiting for transfers between devices, shards(): grad_in_own = lax.psum(grad_in_here.astype(bf16), 'rep').astype(f32)  191 us
    reduce_scatter x1, waiting for transfers between devices, reduce_joint(): part = lax.psum_scatter(joint, 'shard', scatter_dimension=0, tiled=True)  76.3 us
    reduce_scatter x1, waiting for transfers between devices, shards(): lax.psum_scatter(combined.astype(bf16), 'shard', scatter_dimension=0, til...  75.3 us
    reduce_scatter x1, waiting for transfers between devices, shards(): lax.psum_scatter(back_rows, 'shard', scatter_dimension=0, tiled=True)  68.4 us
    dot_general x1, matrix products, experts(): jnp.einsum('td,efd->etf', dy_rows, down_w, preferred_element_type=f32)  28.4 us
    unnamed x105, local copies, waits for them, and re-layouts  28 us
    dot_general x1, matrix products, shards(): jnp.einsum('td,etf->edf', second_all, grad_both, preferred_element_type=f32)  24.8 us
  transfers between devices with their start and end apart: 8, of which 8 were waited for; matrix products, arithmetic and copies ran while one was open for 12% of the time, Pallas kernels for 0%

profile of v1, /device:TPU:0, one launch (start us, length us, event | category | flops | bytes accessed | tf_op | source)
XLA Modules:
  0.0 990.5 jit_solution(4883131591927317545)
XLA Ops:
  18.9 81.9 %all-gather.5.cloned.1.call-done = bf16[1024,2176]{1,0:T(8,128)(2,1)} async-done(((bf16[256,2176]{1,0:T(8,128)(2,1)}), bf16[1024,2176]{1,0:T(8,128)(2,1)}) %all-gather.5.cloned.1.call-update) | async-done | bytes 4456464 | tf_op jit(solution)/shard_map/all_gather | solution.py:120
  102.3 4.8 fusion.24
  118.9 7.7 fusion.70
  126.6 8.3 fusion.6
  135.6 8.7 fusion.41
  146.8 3.3 multiply_reduce_fusion.2
  151.5 85.6 %all-gather.11.cloned.1.call-done = bf16[2048,1152]{0,1:T(8,128)(2,1)} async-done(((bf16[512,1152]{0,1:T(8,128)(2,1)}), bf16[2048,1152]{0,1:T(8,128)(2,1)}) %all-gather.11.cloned.1.call-update) | async-done | bytes 4718608 | tf_op jit(solution)/shard_map/all_gather | solution.py:120
  237.1 81.2 %all-gather.9.cloned.1.call-done = bf16[2048,1024]{0,1:T(8,128)(2,1)} async-done(((bf16[512,1024]{0,1:T(8,128)(2,1)}), bf16[2048,1024]{0,1:T(8,128)(2,1)}) %all-gather.9.cloned.1.call-update) | async-done | bytes 4194320 | tf_op jit(solution)/shard_map/all_gather | solution.py:120
  323.3 23.1 %convolution_bitcast_fusion = f32[4,2048,1024]{1,2,0:T(8,128)} fusion(bf16[4,1024,1024]{2,1,0:T(8,128)(2,1)} %param.31, bf16[2048,1024]{0,1:T(8,128)(2,1)S(1)} %copy-done.9), kind=kOutput, calls=%fused_computation.2 | convolution fusion | flops 17179869184 | bytes 46137344 | tf_op jit(solution)/shard_map/td,edf->etf/dot_general | solution.py:317
  346.4 28.4 %multiply_convert_fusion.1 = (bf16[4,2048,512]{1,2,0:T(8,128)(2,1)}, bf16[4,2048,512]{1,2,0:T(8,128)(2,1)}, f32[4,2048]{1,0:T(4,128)S(1)}, bf16[4,2048,512]{1,2,0:T(8,128)(2,1)}) fusion(f32[4,2048,1024]{1,2,0:T(8,128)} %convolution_bitcast_fusion, f32[4,2048]{1,0:T(4,128)S(1)} %dynamic-slice_bitcast_fusion, bf16[4,512,1024]{2,1,0:T(8,128)(2,1)} %param.32, ...), kind=kOutput, calls=%fused_computation.15 | convolution fusion | flops 8669618176 | bytes 67174400 | tf_op jit(solution)/shard_map/td,efd->etf/dot_general | solution.py:323
  374.8 22.7 %bitcast_convert_fusion = bf16[2048,1024]{0,1:T(8,128)(2,1)S(1)} fusion(bf16[4,1024,1024]{2,1,0:T(8,128)(2,1)} %param.31, bf16[4,2048,512]{1,2,0:T(8,128)(2,1)} %get-tuple-element.122, bf16[4,2048,512]{1,2,0:T(8,128)(2,1)} %get-tuple-element.121), kind=kOutput, calls=%fused_computation.26 | convolution fusion | flops 17215520768 | bytes 29360128 | tf_op jit(solution)/shard_map/etf,edf->td/dot_general | solution.py:212
  397.6 6.7 maximum_maximum_fusion
  404.4 14.1 %bitcast_convert_fusion.1 = bf16[2048,1024]{0,1:T(8,128)(2,1)} fusion(bf16[4,512,1024]{2,1,0:T(8,128)(2,1)} %param.32, bf16[4,2048,512]{1,2,0:T(8,128)(2,1)} %get-tuple-element.124, f32[4,2048]{1,0:T(4,128)S(1)} %dynamic-slice_bitcast_fusion), kind=kOutput, calls=%fused_computation.27 | convolution fusion | flops 8604614656 | bytes 16809984 | tf_op jit(solution)/shard_map/etf,efd->td/dot_general | solution.py:208
  419.9 68.4 %reduce-scatter.6.cloned.1.call-done = bf16[512,1152]{0,1:T(8,128)(2,1)} async-done(((bf16[2048,1152]{0,1:T(8,128)(2,1)}), bf16[512,1152]{0,1:T(8,128)(2,1)}) %reduce-scatter.6.cloned.1.call-update) | async-done | bytes 1179664 | tf_op jit(solution)/shard_map/reduce_scatter | solution.py:230
  489.1 3.3 multiply_reduce_fusion
  492.4 75.3 %reduce-scatter.4.cloned.1.call-done = bf16[512,1024]{0,1:T(8,128)(2,1)} async-done(((bf16[2048,1024]{0,1:T(8,128)(2,1)}), bf16[512,1024]{0,1:T(8,128)(2,1)}) %reduce-scatter.4.cloned.1.call-update) | async-done | bytes 1048592 | tf_op jit(solution)/shard_map/reduce_scatter | solution.py:209
  567.7 3.6 multiply_add_fusion
  574.8 15.1 %fusion.2 = (f32[8,2,512]{2,1,0:T(2,128)S(1)}, f32[8,512,512,2]{2,1,3,0:T(8,128)}) fusion(f32[8,2,512,512]{2,3,1,0:T(8,128)} %get-tuple-element.142, f32[8,2,512]{2,1,0:T(2,128)} %bitcast.136, bf16[512,8,64,1]{0,2,3,1:T(8,128)(2,1)S(1)} %bitcast.125, bf16[512,8,2,64]{0,3,2,1:T(8,128)(2,1)S(1)} %bitcast.119), kind=kOutput, calls=%fused_computation.8 | convolution fusion | flops 549445632 | bytes 35192832 | tf_op jit(solution)/shard_map/qgrd,kgd->grqk/dot_general | solution.py:95
  591.2 8.3 fusion.4
  599.6 3.4 copy-done
  605.8 6.0 fusion.46
  611.8 3.6 fusion.47
  615.5 4.7 convolution_convert_fusion.1
  622.4 4.4 convolution_convert_fusion
  626.9 5.0 fusion.39
  634.6 10.6 %concatenate.62 = bf16[1024,3200]{1,0:T(8,128)(2,1)} concatenate(bf16[1024,2048]{1,0:T(8,128)(2,1)} %convolution_convert_fusion, bf16[1024,1024]{1,0:T(8,128)(2,1)S(1)} %copy-done.17, bf16[1024,16]{1,0:T(8,128)(2,1)} %copy.153, bf16[1024,1]{1,0:T(8,128)(2,1)S(1)} %convert_element_type.230, bf16[1024,1]{1,0:T(8,128)(2,1)} %convert_element_type.231, bf16[1024,110]{1,0:T(8,128)(2,1)} %broadcast_in_dim.43), dimensions={1} | concatenate | bytes 13107200 | tf_op jit(solution)/shard_map/concatenate | solution.py:278
  646.0 13.8 %fusion.31 = bf16[4,512,1024]{2,1,0:T(8,128)(2,1)} fusion(bf16[2048,1152]{0,1:T(8,128)(2,1)} %all-gather.11.cloned.1.call-done, bf16[4,2048,512]{1,2,0:T(8,128)(2,1)} %get-tuple-element.124, f32[4,2048]{1,0:T(4,128)S(1)} %copy-done.36), kind=kOutput, calls=%fused_computation.50 | convolution fusion | flops 8604614656 | bytes 16809984 | tf_op jit(solution)/shard_map/etf,td->efd/dot_general | solution.py:232
  659.8 24.8 %convert_bitcast_fusion = bf16[4,1024,1024]{1,2,0:T(8,128)(2,1)} fusion(bf16[4,2048,512]{1,2,0:T(8,128)(2,1)} %get-tuple-element.122, bf16[4,2048,512]{1,2,0:T(8,128)(2,1)} %get-tuple-element.121, bf16[2048,1024]{0,1:T(8,128)(2,1)} %all-gather.9.cloned.1.call-done), kind=kOutput, calls=%fused_computation.28 | convolution fusion | flops 17217617920 | bytes 29360128 | tf_op jit(solution)/shard_map/td,etf->edf/dot_general | solution.py:231
  684.6 76.3 %reduce-scatter.8.cloned.1.call-done = bf16[256,3200]{1,0:T(8,128)(2,1)} async-done(((bf16[1024,3200]{1,0:T(8,128)(2,1)}), bf16[256,3200]{1,0:T(8,128)(2,1)}) %reduce-scatter.8.cloned.1.call-update) | async-done | bytes 1638416 | tf_op jit(solution)/shard_map/reduce_scatter | solution.py:311
  766.8 191.1 %all-reduce.3.cloned.1.call-done = (bf16[4,1024,1024]{1,2,0:T(8,128)(2,1)}, bf16[256,3200]{1,0:T(8,128)(2,1)}, bf16[4,512,1024]{2,1,0:T(8,128)(2,1)}) async-done(((bf16[4,1024,1024]{1,2,0:T(8,128)(2,1)}, bf16[256,3200]{1,0:T(8,128)(2,1)}, bf16[4,512,1024]{2,1,0:T(8,128)(2,1)}), (bf16[4,1024,1024]{1,2,0:T(8,128)(2,1)}, bf16[256,3200]{1,0:T(8,128)(2,1)}, ...) | async-done | bytes 14221328 | tf_op jit(solution)/shard_map/psum | solution.py:233
  962.6 12.5 %copy.161 = f32[4,1024,1024]{2,1,0:T(8,128)} copy(bf16[4,1024,1024]{1,2,0:T(8,128)(2,1)} %get-tuple-element.114) | data formatting | bytes 25165824
  975.1 6.6 convert_element_type.227
  (187 shorter events, 61.7 us)
Async XLA Ops:
  7.2 6.5 copy-start.22
  7.2 7.0 copy-start.39
  7.2 93.6 %all-gather.5.cloned.1.call-start = ((), (), s32[]{:S(2)}) async-start(), calls=%async_computation.3 | async-start | bytes 5570560 | tf_op jit(solution)/shard_map/all_gather | solution.py:120
  12.8 134.0 %all-gather.7.cloned.1.call-start = ((), (), s32[]{:S(2)}) async-start(), calls=%async_computation.4 | async-start | bytes 2621440 | tf_op jit(solution)/shard_map/all_gather | solution.py:120
  13.6 223.5 %all-gather.11.cloned.1.call-start = ((), (), s32[]{:S(2)}) async-start(), calls=%async_computation.6 | async-start | bytes 5898240 | tf_op jit(solution)/shard_map/all_gather | solution.py:120
  14.2 92.8 %copy-start.5 = (bf16[512,1024]{0,1:T(8,128)(2,1)}, bf16[512,1024]{0,1:T(8,128)(2,1)S(1)}, u32[]{:S(2)}) copy-start(bf16[512,1024]{0,1:T(8,128)(2,1)S(1)} %copy.139) | copy-start | bytes 3145732
  15.7 302.6 %all-gather.9.cloned.1.call-start = ((), (), s32[]{:S(2)}) async-start(), calls=%async_computation.5 | async-start | bytes 5242880 | tf_op jit(solution)/shard_map/all_gather | solution.py:120
  17.3 129.5 %copy-start.3 = (bf16[512,1024]{0,1:T(8,128)(2,1)}, bf16[512,1024]{0,1:T(8,128)(2,1)S(1)}, u32[]{:S(2)}) copy-start(bf16[512,1024]{0,1:T(8,128)(2,1)S(1)} %copy.128) | copy-start | bytes 3145732
  18.3 88.8 %copy-start.40 = (f32[512]{0:T(512)}, f32[512]{0:T(512)S(1)}, u32[]{:S(2)}) copy-start(f32[512]{0:T(512)S(1)} %add_rsqrt_fusion.1) | copy-start | bytes 6148
  18.7 99.8 %copy-start.18 = (f32[512,32]{0,1:T(8,128)}, f32[512,32]{0,1:T(8,128)S(1)}, u32[]{:S(2)}) copy-start(f32[512,32]{0,1:T(8,128)S(1)} %get-tuple-element.139) | copy-start | bytes 196612
  18.7 99.8 %copy-start.20 = (f32[512,32]{0,1:T(8,128)}, f32[512,32]{0,1:T(8,128)S(1)}, u32[]{:S(2)}) copy-start(f32[512,32]{0,1:T(8,128)S(1)} %get-tuple-element.140) | copy-start | bytes 196612
  118.5 8.1 copy-start.23
  118.5 8.1 copy-start.25
  118.8 7.7 copy-start.13
  118.9 7.7 copy-start.15
  126.6 8.4 copy-start.29
  126.6 9.0 copy-start.11
  151.3 336.9 %reduce-scatter.6.cloned.1.call-start = ((), (), s32[]{:S(2)}) async-start(), calls=%async_computation.8 | async-start | bytes 5898240 | tf_op jit(solution)/shard_map/reduce_scatter | solution.py:230
  323.3 81.1 %copy-start.35 = (f32[4,2048]{1,0:T(4,128)}, f32[4,2048]{1,0:T(4,128)S(1)}, u32[]{:S(2)}) copy-start(f32[4,2048]{1,0:T(4,128)S(1)} %dynamic-slice_bitcast_fusion) | copy-start | bytes 98308
  404.3 163.4 %reduce-scatter.4.cloned.1.call-start = ((), (), s32[]{:S(2)}) async-start(), calls=%async_computation.7 | async-start | bytes 5242880 | tf_op jit(solution)/shard_map/reduce_scatter | solution.py:209
  418.5 149.3 %copy-start.6 = (bf16[512,1024]{0,1:T(8,128)(2,1)S(1)}, bf16[512,1024]{0,1:T(8,128)(2,1)}, u32[]{:S(2)}) copy-start(bf16[512,1024]{0,1:T(8,128)(2,1)} %copy-done.5) | copy-start | bytes 3145732
  418.5 342.5 %reduce-scatter.8.cloned.1.call-start = ((), (), s32[]{:S(2)}) async-start(), calls=%async_computation.9 | async-start | bytes 8192000 | tf_op jit(solution)/shard_map/reduce_scatter | solution.py:311
  574.7 15.1 %slice-start = ((s8[16777216]{0:T(1024)(128)(4,1)}), s8[4194304]{0:T(1024)(128)(4,1)S(1)}, s32[]{:S(2)}) async-start(s8[16777216]{0:T(1024)(128)(4,1)} %bitcast.117), calls=%async_computation.11 | async-start | bytes 8388608
  574.8 15.1 %slice-start.1 = ((s8[16777216]{0:T(1024)(128)(4,1)}), s8[4194304]{0:T(1024)(128)(4,1)S(1)}, s32[]{:S(2)}) async-start(s8[16777216]{0:T(1024)(128)(4,1)} %bitcast.117), calls=%async_computation.12 | async-start | bytes 8388608
  574.8 15.1 %slice-start.2 = ((s8[16777216]{0:T(1024)(128)(4,1)}), s8[4194304]{0:T(1024)(128)(4,1)S(1)}, s32[]{:S(2)}) async-start(s8[16777216]{0:T(1024)(128)(4,1)} %bitcast.117), calls=%async_computation.13 | async-start | bytes 8388608
  574.8 16.4 %slice-start.3 = ((s8[16777216]{0:T(1024)(128)(4,1)}), s8[4194304]{0:T(1024)(128)(4,1)S(1)}, s32[]{:S(2)}) async-start(s8[16777216]{0:T(1024)(128)(4,1)} %bitcast.117), calls=%async_computation.14 | async-start | bytes 8388608
  574.8 16.4 %copy-start.28 = (f32[2,8,512]{2,1,0:T(8,128)S(1)}, f32[2,8,512]{2,1,0:T(8,128)}, u32[]{:S(2)}) copy-start(f32[2,8,512]{2,1,0:T(8,128)} %log_add_fusion) | copy-start | bytes 98308
  591.2 11.7 %copy-start.24 = (bf16[512,8,32]{0,2,1:T(8,128)(2,1)S(1)}, bf16[512,8,32]{0,2,1:T(8,128)(2,1)}, u32[]{:S(2)}) copy-start(bf16[512,8,32]{0,2,1:T(8,128)(2,1)} %copy-done.23) | copy-start | bytes 786436
  591.2 11.7 %copy-start.26 = (bf16[512,8,32]{0,2,1:T(8,128)(2,1)S(1)}, bf16[512,8,32]{0,2,1:T(8,128)(2,1)}, u32[]{:S(2)}) copy-start(bf16[512,8,32]{0,2,1:T(8,128)(2,1)} %copy-done.25) | copy-start | bytes 786436
  615.4 6.5 copy-start.27
  626.9 7.7 copy-start.17
  645.3 312.7 %all-reduce.3.cloned.1.call-start = ((), (), s32[]{:S(2)}) async-start(), calls=%async_computation.10 | async-start | bytes 28442624 | tf_op jit(solution)/shard_map/psum | solution.py:233
  (25 other events, 79.4 us)
Sparse Core Ops, SparseCore 0:
  12.9 87.7 all-gather.4
  102.3 44.4 all-gather.6
  149.0 88.1 all-gather.10
  239.1 79.1 all-gather.8
  404.4 83.7 reduce-scatter.5
  490.4 77.2 reduce-scatter.3
  645.4 115.4 reduce-scatter.7
  766.1 191.8 all-reduce.2

commit v2 on v1

--- a/solution.py
+++ b/solution.py
@@ -1,6 +1,8 @@
 import jax
 import jax.numpy as jnp
 from jax import lax
+from jax.experimental import pallas as pl
+from jax.experimental.pallas import tpu as pltpu
 from jax.sharding import PartitionSpec as P
 
 HEADS = 16
@@ -8,6 +10,7 @@
 HEAD_DIM = 64
 EXPERTS = 16
 PAD = 128
+VMEM_BYTES = 54 * 2**20
 
 
 epsilon = 1e-06
@@ -114,6 +117,235 @@
         )
     )
     return (query_parts, grad_key, grad_value)
+
+
+MESH = pl.DeviceIdType.MESH
+HALVES = 2
+
+
+def bit_orders(reps):
+    bits = reps.bit_length() - 1
+    first = list(range(bits))
+    return (first, first[:1] + first[1:][::-1])
+
+
+def rep_place(rep_at, order):
+    place = 0
+    for bit in order:
+        place = place * 2 + rep_at // 2**bit % 2
+    return place
+
+
+def partner(rep_at, bit):
+    return rep_at + 2**bit * (1 - 2 * (rep_at // 2**bit % 2))
+
+
+def halves_of(columns):
+    tiles = columns // 128
+    left = (tiles + 1) // 2 * 128
+    return (pl.ds(0, left), pl.ds(left, columns - left))
+
+
+def meet(rep_at, shard_at, reps, shard_count):
+    barrier = pltpu.get_barrier_semaphore()
+    bits = reps.bit_length() - 1
+    for bit in range(bits):
+        pl.semaphore_signal(
+            barrier, inc=1, device_id=(partner(rep_at, bit), shard_at), device_id_type=MESH
+        )
+    for step in range(1, shard_count):
+        pl.semaphore_signal(
+            barrier,
+            inc=1,
+            device_id=(rep_at, (shard_at + step) % shard_count),
+            device_id_type=MESH,
+        )
+    pl.semaphore_wait(barrier, bits + shard_count - 1)
+
+
+def spread(out, orders, columns, rep_at, shard_at, sends, recvs):
+    bits = len(orders[0])
+    flying = [None] * HALVES
+    for at in reversed(range(bits)):
+        window = 2 ** (bits - 1 - at)
+        for half in range(HALVES):
+            order = orders[half]
+            place = rep_place(rep_at, order)
+            begin = place // window * window
+            if flying[half] is not None:
+                flying[half].wait()
+            block = out.at[:, pl.ds(begin, window), :, columns[half]]
+            flying[half] = pltpu.make_async_remote_copy(
+                src_ref=block,
+                dst_ref=block,
+                send_sem=sends.at[half, at],
+                recv_sem=recvs.at[half, at],
+                device_id=(partner(rep_at, order[at]), shard_at),
+                device_id_type=MESH,
+            )
+            flying[half].start()
+    for half in range(HALVES):
+        flying[half].wait()
+
+
+def gather_kernel(reps, shard_count, piece, out, z_send, z_recv, sends, recvs):
+    rep_at, shard_at = (lax.axis_index("rep"), lax.axis_index("shard"))
+    orders = bit_orders(reps)
+    columns = halves_of(piece.shape[-1])
+    meet(rep_at, shard_at, reps, shard_count)
+    flying = []
+    for half in range(HALVES):
+        place = rep_place(rep_at, orders[half])
+        for step in range(1, shard_count):
+            copy = pltpu.make_async_remote_copy(
+                src_ref=piece.at[place, :, columns[half]],
+                dst_ref=out.at[shard_at, place, :, columns[half]],
+                send_sem=z_send.at[half, step - 1],
+                recv_sem=z_recv.at[half, step - 1],
+                device_id=(rep_at, (shard_at + step) % shard_count),
+                device_id_type=MESH,
+            )
+            copy.start()
+            flying.append(copy)
+        out[shard_at, place, :, columns[half]] = piece[place, :, columns[half]]
+    for copy in flying:
+        copy.wait()
+    spread(out, orders, columns, rep_at, shard_at, sends, recvs)
+
+
+def gather_all(piece, reps, shard_count, number):
+    own, width = piece.shape
+    rows = own // reps
+    bits = reps.bit_length() - 1
+    out = pl.pallas_call(
+        lambda *refs: gather_kernel(reps, shard_count, *refs),
+        out_shape=jax.ShapeDtypeStruct((shard_count, reps, rows, width), piece.dtype),
+        in_specs=[pl.BlockSpec(memory_space=pltpu.VMEM)],
+        out_specs=pl.BlockSpec(memory_space=pltpu.VMEM),
+        scratch_shapes=[
+            pltpu.SemaphoreType.DMA((HALVES, shard_count)),
+            pltpu.SemaphoreType.DMA((HALVES, shard_count)),
+            pltpu.SemaphoreType.DMA((HALVES, bits)),
+            pltpu.SemaphoreType.DMA((HALVES, bits)),
+        ],
+        compiler_params=pltpu.CompilerParams(
+            collective_id=number, has_side_effects=True, vmem_limit_bytes=VMEM_BYTES
+        ),
+        cost_estimate=pl.CostEstimate(
+            flops=0, bytes_accessed=16 * shard_count * own * width, transcendentals=0
+        ),
+    )(piece.reshape(reps, rows, width))
+    return out.reshape(shard_count * own, width)
+
+
+def reduce_kernel(reps, shard_count, parts, out, *scratch):
+    bits = reps.bit_length() - 1
+    f32 = jnp.float32
+    landed = [scratch[half * bits : (half + 1) * bits] for half in range(HALVES)]
+    rest = scratch[HALVES * bits :]
+    if shard_count > 1:
+        z_land, (z_send, z_recv) = (rest[:HALVES], rest[HALVES : HALVES + 2])
+        rest = rest[HALVES + 2 :]
+    r_send, r_recv, sends, recvs = rest
+    rep_at, shard_at = (lax.axis_index("rep"), lax.axis_index("shard"))
+    orders = bit_orders(reps)
+    columns = halves_of(parts.shape[-1])
+    meet(rep_at, shard_at, reps, shard_count)
+    flying = [None] * HALVES
+
+    def source(half, at):
+        return parts.at[:, :, :, columns[half]] if at == 0 else landed[half][at - 1]
+
+    def begin(half, at):
+        bit = orders[half][at]
+        many = reps // 2 ** (at + 1)
+        away = (1 - rep_at // 2**bit % 2) * many
+        flying[half] = pltpu.make_async_remote_copy(
+            src_ref=source(half, at).at[:, pl.ds(away, many)],
+            dst_ref=landed[half][at],
+            send_sem=r_send.at[half, at],
+            recv_sem=r_recv.at[half, at],
+            device_id=(partner(rep_at, bit), shard_at),
+            device_id_type=MESH,
+        )
+        flying[half].start()
+
+    for half in range(HALVES):
+        begin(half, 0)
+    for at in range(bits):
+        many = reps // 2 ** (at + 1)
+        for half in range(HALVES):
+            flying[half].wait()
+            keep = rep_at // 2 ** orders[half][at] % 2 * many
+            mine, came = (source(half, at), landed[half][at])
+
+            @pl.loop(0, parts.shape[0] * many)
+            def _(index):
+                outer, inner = (index // many, index % many)
+                came[outer, inner] = (
+                    came[outer, inner].astype(f32) + mine[outer, keep + inner].astype(f32)
+                ).astype(came.dtype)
+
+            if at + 1 < bits:
+                begin(half, at + 1)
+    copies = []
+    if shard_count > 1:
+        for half in range(HALVES):
+            for step in range(1, shard_count):
+                to = (shard_at + step) % shard_count
+                copy = pltpu.make_async_remote_copy(
+                    src_ref=landed[half][-1].at[to, 0],
+                    dst_ref=z_land[half].at[step - 1],
+                    send_sem=z_send.at[half, step - 1],
+                    recv_sem=z_recv.at[half, step - 1],
+                    device_id=(rep_at, to),
+                    device_id_type=MESH,
+                )
+                copy.start()
+                copies.append(copy)
+    for copy in copies:
+        copy.wait()
+    for half in range(HALVES):
+        place = rep_place(rep_at, orders[half])
+        if shard_count > 1:
+            total = landed[half][-1][shard_at, 0].astype(f32)
+            for step in range(1, shard_count):
+                total = total + z_land[half][step - 1].astype(f32)
+            out[0, place, :, columns[half]] = total.astype(out.dtype)
+        else:
+            out[0, place, :, columns[half]] = landed[half][-1][0, 0]
+    spread(out, orders, columns, rep_at, shard_at, sends, recvs)
+
+
+def reduce_all(parts, reps, shard_count, number):
+    total, width = parts.shape
+    rows = total // (reps * shard_count)
+    bits = reps.bit_length() - 1
+    widths = (halves_of(width)[0].size, halves_of(width)[1].size)
+    scratch = []
+    for wide in widths:
+        for at in range(bits):
+            scratch.append(
+                pltpu.VMEM((shard_count, reps // 2 ** (at + 1), rows, wide), parts.dtype)
+            )
+    if shard_count > 1:
+        scratch += [pltpu.VMEM((shard_count - 1, rows, wide), parts.dtype) for wide in widths]
+        scratch += [pltpu.SemaphoreType.DMA((HALVES, shard_count)) for _ in range(2)]
+    scratch += [pltpu.SemaphoreType.DMA((HALVES, bits)) for _ in range(4)]
+    out = pl.pallas_call(
+        lambda *refs: reduce_kernel(reps, shard_count, *refs),
+        out_shape=jax.ShapeDtypeStruct((1, reps, rows, width), parts.dtype),
+        in_specs=[pl.BlockSpec(memory_space=pltpu.VMEM)],
+        out_specs=pl.BlockSpec(memory_space=pltpu.VMEM),
+        scratch_shapes=scratch,
+        compiler_params=pltpu.CompilerParams(
+            collective_id=number, has_side_effects=True, vmem_limit_bytes=VMEM_BYTES
+        ),
+        cost_estimate=pl.CostEstimate(
+            flops=0, bytes_accessed=32 * total * width, transcendentals=0
+        ),
+    )(parts.reshape(shard_count, reps, rows, width))
+    return out.reshape(reps * rows, width)
 
 
 def gather_shard(piece):
@@ -153,13 +385,17 @@
         ],
         axis=1,
     )
-    qkv_full = gather_shard(jnp.concatenate([w_query, w_key, w_value, small], axis=1))
-    qkv_w = qkv_full[:, : query_cols + 2 * kv_cols]
-    small_full = qkv_full[:, query_cols + 2 * kv_cols :]
+    reps, shard_count = (lax.axis_size("rep"), lax.axis_size("shard"))
+    all_w = gather_all(
+        jnp.concatenate([w_query, w_key, w_value, w_out, small], axis=1), reps, shard_count, 1
+    )
+    qkv_cols = query_cols + 2 * kv_cols
+    qkv_w = all_w[:, :qkv_cols]
+    out_w = all_w[:, qkv_cols : qkv_cols + w_out.shape[1]]
+    small_full = all_w[:, qkv_cols + w_out.shape[1] :]
     router_full = small_full[:, :EXPERTS]
     gain_in = small_full[:, EXPERTS].astype(f32)
     gain_mid = small_full[:, EXPERTS + 1].astype(f32)
-    out_w = gather_shard(w_out)
     mask_own = jnp.any(
         routes[:, :, None] == jnp.arange(EXPERTS, dtype=jnp.int32)[None, None, :], axis=1
     )
@@ -230,8 +466,12 @@
     back_own = lax.psum_scatter(back_rows, "shard", scatter_dimension=0, tiled=True)
     grad_in_here = jnp.einsum("td,etf->edf", second_all, grad_both, preferred_element_type=f32)
     grad_down_here = jnp.einsum("etf,td->efd", gated, dy_all, preferred_element_type=f32)
-    grad_in_own = lax.psum(grad_in_here.astype(bf16), "rep").astype(f32)
-    grad_down_own = lax.psum(grad_down_here.astype(bf16), "rep").astype(f32)
+    expert_grads = jnp.concatenate([grad_in_here.astype(bf16), grad_down_here.astype(bf16)], axis=1)
+    expert_own = reduce_all(expert_grads.reshape(-1, model_width), reps, 1, 2)
+    back_own, expert_own = lax.optimization_barrier((back_own, expert_own))
+    expert_own = expert_own.reshape(expert_grads.shape)
+    grad_in_own = expert_own[:, :model_width].astype(f32)
+    grad_down_own = expert_own[:, model_width:].astype(f32)
 
     mixed = (middle + combined_own.astype(f32)).astype(bf16)
     gate_back = back_own[:, model_width : model_width + 2 * EXPERTS].astype(f32)
@@ -286,7 +526,7 @@
         ],
         axis=1,
     )
-    joint_own = reduce_joint(joint).astype(f32)
+    joint_own = reduce_all(joint, reps, shard_count, 3).astype(f32)
     edges = [0]
     for width in (query_cols, kv_cols, kv_cols, w_out.shape[1], EXPERTS, 1, 1):
         edges.append(edges[-1] + width)
@@ -307,11 +547,6 @@
     )
 
 
-def reduce_joint(joint):
-    part = lax.psum_scatter(joint, "shard", scatter_dimension=0, tiled=True)
-    return lax.psum(part, "rep")
-
-
 def experts(rows, dy_rows, gates, in_w, down_w):
     f32, bf16 = jnp.float32, jnp.bfloat16
     both = jnp.einsum("td,edf->etf", rows, in_w, preferred_element_type=f32)

time: 1000 us -> 768 us (0.77)
  waiting for transfers between devices: 663 us -> 142 us
  Pallas kernels: 0 us -> 272 us
  other arithmetic: 49.2 us -> 75 us
  local copies, waits for them, and re-layouts: 60.7 us -> 49 us
    pallas_call x0 -> x3, Pallas kernels: none -> 272 us  [the longest x2 210 us: reduce_all(): pl.pallas_call(lambda *refs: reduce_kernel(reps, shard_count, *refs), out...]
    psum x1 -> x0, waiting for transfers between devices: 191 us -> none  [shards(): grad_in_own = lax.psum(grad_in_here.astype(bf16), 'rep').astype(f32)]
    all_gather x4 -> x2, waiting for transfers between devices: 251 us -> 142 us  [gather_shard(): return lax.all_gather(piece, 'shard', axis=0, tiled=True)]
    reduce_scatter x1 -> x0, waiting for transfers between devices: 76.3 us -> none  [reduce_joint(): part = lax.psum_scatter(joint, 'shard', scatter_dimension=0, tiled=True)]
    reduce_scatter x1, waiting for transfers between devices: 75.3 us -> 0.01 us  [shards(): lax.psum_scatter(combined.astype(bf16), 'shard', scatter_dimension=0, til...]
    reduce_scatter x1, waiting for transfers between devices: 68.4 us -> 0.02 us  [shards(): lax.psum_scatter(back_rows, 'shard', scatter_dimension=0, tiled=True)]
    concatenate x0 -> x1, other arithmetic: none -> 13.3 us  [shards(): jnp.concatenate([grad_in_here.astype(bf16), grad_down_here.astype(bf16)],...]
    unnamed x105 -> x110, local copies, waits for them, and re-layouts: 28 us -> 15.9 us
  transfers between devices with their start and end apart: 8 -> 4, of which waited for: 8 -> 2; matrix products, arithmetic and copies ran while one was open for 12% -> 13% of each run, Pallas kernels for 0% -> 18%
where the time goes in v2:
time: 768 us; the launch traced here: 758 us
  Pallas kernels  272 us (35%)
  matrix products  206 us (27%)
  waiting for transfers between devices  142 us (18%)
  other arithmetic  75 us (10%)
  local copies, waits for them, and re-layouts  49 us (6%)
  between operations  14.8 us (2%)
    pallas_call x2, Pallas kernels, reduce_all(): pl.pallas_call(lambda *refs: reduce_kernel(reps, shard_count, *refs), out...  210 us
    all_gather x2, waiting for transfers between devices, gather_shard(): return lax.all_gather(piece, 'shard', axis=0, tiled=True)  142 us
    pallas_call x1, Pallas kernels, gather_all(): pl.pallas_call(lambda *refs: gather_kernel(reps, shard_count, *refs), out...  61.6 us
    dot_general x1, matrix products, experts(): jnp.einsum('td,efd->etf', dy_rows, down_w, preferred_element_type=f32)  28.4 us
    dot_general x1, matrix products, experts(): both = jnp.einsum('td,edf->etf', rows, in_w, preferred_element_type=f32)  25.3 us
    dot_general x1, matrix products, shards(): jnp.einsum('td,etf->edf', second_all, grad_both, preferred_element_type=f32)  24.5 us
    dot_general x1, matrix products, shards(): jnp.einsum('etf,edf->td', grad_both, w_expert_in, preferred_element_type=...  22.9 us
    unnamed x110, local copies, waits for them, and re-layouts  15.9 us
  transfers between devices with their start and end apart: 4, of which 2 were waited for; matrix products, arithmetic and copies ran while one was open for 13% of the time, Pallas kernels for 18%

profile of v2, /device:TPU:0, one launch (start us, length us, event | category | flops | bytes accessed | tf_op | source)
XLA Modules:
  0.0 757.9 jit_solution(7413480688803308159)
XLA Ops:
  9.9 3.8 concatenate.81.refs_0_
  13.7 61.6 %shard_map.222 = bf16[4,8,32,3200]{3,2,1,0:T(8,128)(2,1)} custom-call(bf16[8,32,3200]{2,1,0:T(8,128)(2,1)} %concatenate.81.refs_0_), custom_call_target="tpu_custom_call" | custom-call | bytes 52428800 | tf_op jit(solution)/shard_map/pallas_call | solution.py:220
  78.4 4.8 fusion.24
  96.8 9.0 %fusion.79 = (f32[8,2,512]{2,1,0:T(2,128)S(1)}, f32[8,2,512,512]{2,3,1,0:T(8,128)}) fusion(bf16[512,8,2,32]{0,3,2,1:T(8,128)(2,1)} %bitcast.156, bf16[512,8,2,32]{0,3,2,1:T(8,128)(2,1)} %bitcast.154, bf16[512,8,32]{0,2,1:T(8,128)(2,1)S(1)} %get-tuple-element.95, bf16[512,8,32]{0,2,1:T(8,128)(2,1)S(1)} %get-tuple-element.94, pred[512,512]{0,1:T(8,128)(4,1)S(1)} %fusion.59), kind=kOutput, calls=%fused_computation.145 | convolution fusion | flops 552591360 | bytes 18644992 | tf_op jit(solution)/shard_map/qgrd,kgd->grqk/dot_general | solution.py:66
  105.8 8.2 %fusion.6 = f32[8,2,512]{2,1,0:T(2,128)S(1)} fusion(f32[8,2,512,512]{2,3,1,0:T(8,128)} %get-tuple-element.99, f32[8,2,512]{2,1,0:T(2,128)S(1)} %get-tuple-element.98), kind=kLoop, calls=%fused_computation.21 | loop fusion | flops 8380416 | bytes 16842752 | tf_op jit(solution)/shard_map/reduce_sum | solution.py:81
  114.0 8.0 %fusion.47 = bf16[8,64,2,512]{3,1,2,0:T(8,128)(2,1)S(1)} fusion(bf16[512,8,64,1]{0,2,3,1:T(8,128)(2,1)S(1)} %bitcast.152, f32[8,2,512,512]{2,3,1,0:T(8,128)} %get-tuple-element.99, f32[8,2,512]{2,1,0:T(2,128)S(1)} %fusion.6, f32[8,2,512]{2,1,0:T(2,128)S(1)} %get-tuple-element.98), kind=kOutput, calls=%fused_computation.77 | convolution fusion | flops 549978112 | bytes 18415616 | tf_op jit(solution)/shard_map/grqk,kgd->qgrd/dot_general | solution.py:83
  122.1 3.3 multiply_reduce_fusion.2
  131.6 76.7 %all-gather.3.cloned.1.call-done = bf16[2048,1024]{0,1:T(8,128)(2,1)} async-done(((bf16[512,1024]{0,1:T(8,128)(2,1)}), bf16[2048,1024]{0,1:T(8,128)(2,1)}) %all-gather.3.cloned.1.call-update) | async-done | bytes 4194320 | tf_op jit(solution)/shard_map/all_gather | solution.py:352
  208.3 25.3 %convolution_bitcast_fusion = f32[4,2048,1024]{1,2,0:T(8,128)} fusion(bf16[4,1024,1024]{2,1,0:T(8,128)(2,1)} %param.31, bf16[2048,1024]{0,1:T(8,128)(2,1)} %all-gather.3.cloned.1.call-done), kind=kOutput, calls=%fused_computation.2 | convolution fusion | flops 17179869184 | bytes 46137344 | tf_op jit(solution)/shard_map/td,edf->etf/dot_general | solution.py:552
  233.5 64.9 %all-gather.5.cloned.1.call-done = bf16[2048,1152]{0,1:T(8,128)(2,1)} async-done(((bf16[512,1152]{0,1:T(8,128)(2,1)}), bf16[2048,1152]{0,1:T(8,128)(2,1)}) %all-gather.5.cloned.1.call-update) | async-done | bytes 4718608 | tf_op jit(solution)/shard_map/all_gather | solution.py:352
  303.9 28.4 %multiply_convert_fusion.1 = (bf16[4,2048,512]{1,2,0:T(8,128)(2,1)}, bf16[4,2048,512]{1,2,0:T(8,128)(2,1)}, f32[4,2048]{1,0:T(4,128)S(1)}, bf16[4,2048,512]{1,2,0:T(8,128)(2,1)}) fusion(f32[4,2048,1024]{1,2,0:T(8,128)} %convolution_bitcast_fusion, f32[4,2048]{1,0:T(4,128)S(1)} %dynamic-slice_bitcast_fusion, bf16[4,512,1024]{2,1,0:T(8,128)(2,1)} %param.32, ...), kind=kOutput, calls=%fused_computation.15 | convolution fusion | flops 8669618176 | bytes 67174400 | tf_op jit(solution)/shard_map/td,efd->etf/dot_general | solution.py:558
  332.3 22.9 %bitcast_convert_fusion = bf16[2048,1024]{0,1:T(8,128)(2,1)S(1)} fusion(bf16[4,1024,1024]{2,1,0:T(8,128)(2,1)} %param.31, bf16[4,2048,512]{1,2,0:T(8,128)(2,1)} %get-tuple-element.77, bf16[4,2048,512]{1,2,0:T(8,128)(2,1)} %get-tuple-element.76), kind=kOutput, calls=%fused_computation.28 | convolution fusion | flops 17215520768 | bytes 29360128 | tf_op jit(solution)/shard_map/etf,edf->td/dot_general | solution.py:448
  355.2 6.3 maximum_maximum_fusion
  361.6 14.0 %bitcast_convert_fusion.1 = bf16[2048,1024]{0,1:T(8,128)(2,1)} fusion(bf16[4,512,1024]{2,1,0:T(8,128)(2,1)} %param.32, bf16[4,2048,512]{1,2,0:T(8,128)(2,1)} %get-tuple-element.79, f32[4,2048]{1,0:T(4,128)S(1)} %dynamic-slice_bitcast_fusion), kind=kOutput, calls=%fused_computation.29 | convolution fusion | flops 8604614656 | bytes 16809984 | tf_op jit(solution)/shard_map/etf,efd->td/dot_general | solution.py:444
  376.3 13.9 %fusion.31 = bf16[4,512,1024]{2,1,0:T(8,128)(2,1)} fusion(bf16[2048,1152]{0,1:T(8,128)(2,1)} %all-gather.5.cloned.1.call-done, bf16[4,2048,512]{1,2,0:T(8,128)(2,1)} %get-tuple-element.79, f32[4,2048]{1,0:T(4,128)S(1)} %dynamic-slice_bitcast_fusion), kind=kOutput, calls=%fused_computation.53 | convolution fusion | flops 8604614656 | bytes 16809984 | tf_op jit(solution)/shard_map/etf,td->efd/dot_general | solution.py:468
  390.1 24.5 %convert_bitcast_fusion = bf16[4,1024,1024]{2,1,0:T(8,128)(2,1)} fusion(bf16[4,2048,512]{1,2,0:T(8,128)(2,1)} %get-tuple-element.77, bf16[4,2048,512]{1,2,0:T(8,128)(2,1)} %get-tuple-element.76, bf16[2048,1024]{0,1:T(8,128)(2,1)} %all-gather.3.cloned.1.call-done), kind=kOutput, calls=%fused_computation.31 | convolution fusion | flops 17217617920 | bytes 29360128 | tf_op jit(solution)/shard_map/td,etf->edf/dot_general | solution.py:467
  414.7 13.3 %pad_maximum_fusion.1 = bf16[4,1536,1024]{2,1,0:T(8,128)(2,1)} fusion(bf16[4,512,1024]{2,1,0:T(8,128)(2,1)} %fusion.31, bf16[4,1024,1024]{2,1,0:T(8,128)(2,1)} %convert_bitcast_fusion), kind=kLoop, calls=%fused_computation.23 | loop fusion | flops 25165824 | bytes 25165824 | tf_op jit(solution)/shard_map/concatenate | solution.py:469
  428.0 139.1 %shard_map.223 = bf16[1,8,768,1024]{3,2,1,0:T(8,128)(2,1)} custom-call(bf16[1,8,768,1024]{3,2,1,0:T(8,128)(2,1)} %bitcast.136), custom_call_target="tpu_custom_call" | custom-call | bytes 201326592 | tf_op jit(solution)/shard_map/pallas_call | solution.py:335
  568.0 3.3 multiply_reduce_fusion
  571.4 3.5 multiply_add_fusion
  579.8 15.1 %fusion.2 = (f32[8,2,512]{2,1,0:T(2,128)S(1)}, f32[8,512,512,2]{2,1,3,0:T(8,128)}) fusion(f32[8,2,512,512]{2,3,1,0:T(8,128)} %get-tuple-element.99, f32[8,2,512]{2,1,0:T(2,128)} %bitcast.168, bf16[512,8,64,1]{0,2,3,1:T(8,128)(2,1)S(1)} %bitcast.153, bf16[512,8,2,64]{0,3,2,1:T(8,128)(2,1)S(1)} %bitcast.137), kind=kOutput, calls=%fused_computation.8 | convolution fusion | flops 549445632 | bytes 35192832 | tf_op jit(solution)/shard_map/qgrd,kgd->grqk/dot_general | solution.py:98
  596.2 8.3 %fusion.4 = bf16[8,2,512,512]{2,3,1,0:T(8,128)(2,1)S(1)} fusion(f32[8,512,512,2]{2,1,3,0:T(8,128)} %get-tuple-element.106, f32[8,2,512,512]{2,3,1,0:T(8,128)S(1)} %bitcast.133, f32[8,2,512]{2,1,0:T(2,128)S(1)} %get-tuple-element.105, f32[8,2,512]{2,1,0:T(2,128)S(1)} %bitcast.170), kind=kLoop, calls=%fused_computation.10 | loop fusion | flops 16777216 | bytes 42008576 | tf_op jit(solution)/shard_map/convert_element_type | solution.py:102
  604.6 3.4 copy-done
  610.8 6.0 fusion.55
  616.8 3.7 fusion.56
  620.6 4.7 convolution_convert_fusion.1
  626.6 4.4 convolution_convert_fusion
  631.0 5.0 fusion.39
  639.6 10.5 %concatenate.98.refs_0_ = bf16[4,8,32,3200]{3,2,1,0:T(8,128)(2,1)} concatenate(bf16[4,8,32,2048]{3,2,1,0:T(8,128)(2,1)} %bitcast.150, bf16[4,8,32,1024]{3,2,1,0:T(8,128)(2,1)S(1)} %bitcast.158, bf16[4,8,32,16]{3,2,1,0:T(8,128)(2,1)} %bitcast.159, bf16[4,8,32,1]{3,2,1,0:T(8,128)(2,1)S(1)} %convert_element_type.237, bf16[4,8,32,1]{3,2,1,0:T(8,128)(2,1)} %convert_element_type.238, ...), dimensions={3} | concatenate | bytes 13107200 | tf_op jit(solution)/shard_map/concatenate | solution.py:518
  650.1 71.0 %shard_map.224 = bf16[1,8,32,3200]{3,2,1,0:T(8,128)(2,1)} custom-call(bf16[4,8,32,3200]{3,2,1,0:T(8,128)(2,1)} %concatenate.98.refs_0_), custom_call_target="tpu_custom_call" | custom-call | bytes 104857600 | tf_op jit(solution)/shard_map/pallas_call | solution.py:335
  726.3 11.7 %slice_convert_fusion = f32[4,1024,1024]{2,1,0:T(8,128)} fusion(bf16[4,1536,1024]{2,1,0:T(8,128)(2,1)} %bitcast.134), kind=kLoop, calls=%fused_computation.27 | loop fusion | flops 4194304 | bytes 25165824 | tf_op jit(solution)/shard_map/convert_element_type | solution.py:473
  738.0 6.6 slice_convert_fusion.1
  (185 shorter events, 57.8 us)
Async XLA Ops:
  7.2 201.1 %all-gather.3.cloned.1.call-start = ((), (), s32[]{:S(2)}) async-start(), calls=%async_computation.2 | async-start | bytes 5242880 | tf_op jit(solution)/shard_map/all_gather | solution.py:352
  13.7 63.9 %copy-start.20 = (bf16[512,1024]{1,0:T(8,128)(2,1)S(1)}, bf16[512,1024]{1,0:T(8,128)(2,1)}, u32[]{:S(2)}) copy-start(bf16[512,1024]{1,0:T(8,128)(2,1)} %param.21) | copy-start | bytes 3145732
  77.5 5.7 copy-start.38
  78.1 44.0 %copy-start.4 = (bf16[512,1024]{0,1:T(8,128)(2,1)}, bf16[512,1024]{0,1:T(8,128)(2,1)S(1)}, u32[]{:S(2)}) copy-start(bf16[512,1024]{0,1:T(8,128)(2,1)S(1)} %copy.134) | copy-start | bytes 3145732
  95.3 10.5 %copy-start.21 = (bf16[512,8,32]{0,2,1:T(8,128)(2,1)}, bf16[512,8,32]{0,2,1:T(8,128)(2,1)S(1)}, u32[]{:S(2)}) copy-start(bf16[512,8,32]{0,2,1:T(8,128)(2,1)S(1)} %get-tuple-element.94) | copy-start | bytes 786436
  95.3 10.5 %copy-start.23 = (bf16[512,8,32]{0,2,1:T(8,128)(2,1)}, bf16[512,8,32]{0,2,1:T(8,128)(2,1)S(1)}, u32[]{:S(2)}) copy-start(bf16[512,8,32]{0,2,1:T(8,128)(2,1)S(1)} %get-tuple-element.95) | copy-start | bytes 786436
  96.7 17.3 %copy-start.11 = (bf16[512,512]{0,1:T(8,128)(2,1)}, bf16[512,512]{0,1:T(8,128)(2,1)S(1)}, u32[]{:S(2)}) copy-start(bf16[512,512]{0,1:T(8,128)(2,1)S(1)} %copy.139) | copy-start | bytes 1572868
  105.8 8.2 %copy-start.29 = (f32[8,2,512]{2,1,0:T(2,128)}, f32[8,2,512]{2,1,0:T(2,128)S(1)}, u32[]{:S(2)}) copy-start(f32[8,2,512]{2,1,0:T(2,128)S(1)} %get-tuple-element.98) | copy-start | bytes 98308
  114.0 8.0 %copy-start.31 = (f32[8,2,512]{2,1,0:T(2,128)}, f32[8,2,512]{2,1,0:T(2,128)S(1)}, u32[]{:S(2)}) copy-start(f32[8,2,512]{2,1,0:T(2,128)S(1)} %fusion.6) | copy-start | bytes 98308
  125.4 6.0 copy-start.1
  128.4 170.0 %all-gather.5.cloned.1.call-start = ((), (), s32[]{:S(2)}) async-start(), calls=%async_computation.3 | async-start | bytes 5898240 | tf_op jit(solution)/shard_map/all_gather | solution.py:352
  129.9 103.6 %copy-start.6 = (bf16[512,1024]{0,1:T(8,128)(2,1)}, bf16[512,1024]{0,1:T(8,128)(2,1)S(1)}, u32[]{:S(2)}) copy-start(bf16[512,1024]{0,1:T(8,128)(2,1)S(1)} %copy.147) | copy-start | bytes 3145732
  131.4 435.7 %reduce-scatter.5.cloned.1.call-start = ((), (), s32[]{:S(2)}) async-start(), calls=%async_computation.5 | async-start | bytes 5898240 | tf_op jit(solution)/shard_map/reduce_scatter | solution.py:466
  361.5 209.8 %reduce-scatter.3.cloned.1.call-start = ((), (), s32[]{:S(2)}) async-start(), calls=%async_computation.4 | async-start | bytes 5242880 | tf_op jit(solution)/shard_map/reduce_scatter | solution.py:445
  361.6 14.1 %copy-start.30 = (f32[8,2,512]{2,1,0:T(2,128)S(1)}, f32[8,2,512]{2,1,0:T(2,128)}, u32[]{:S(2)}) copy-start(f32[8,2,512]{2,1,0:T(2,128)} %copy-done.29) | copy-start | bytes 98308
  361.6 14.1 %copy-start.32 = (f32[8,2,512]{2,1,0:T(2,128)S(1)}, f32[8,2,512]{2,1,0:T(2,128)}, u32[]{:S(2)}) copy-start(f32[8,2,512]{2,1,0:T(2,128)} %copy-done.31) | copy-start | bytes 98308
  428.0 140.0 %copy-start.28 = (f32[2048,16]{0,1:T(8,128)S(1)}, f32[2048,16]{0,1:T(8,128)}, u32[]{:S(2)}) copy-start(f32[2048,16]{0,1:T(8,128)} %copy-done.27) | copy-start | bytes 393220
  428.0 140.0 %copy-start.2 = (f32[512,1024]{0,1:T(8,128)S(1)}, f32[512,1024]{0,1:T(8,128)}, u32[]{:S(2)}) copy-start(f32[512,1024]{0,1:T(8,128)} %copy-done.1) | copy-start | bytes 6291460
  428.0 140.0 %copy-start.34 = (f32[1024,1]{0,1:T(1,128)S(1)}, f32[1024,1]{0,1:T(1,128)}, u32[]{:S(2)}) copy-start(f32[1024,1]{0,1:T(1,128)} %copy-done.33) | copy-start | bytes 12292
  428.0 140.0 %copy-start.37 = (f32[512]{0:T(512)S(1)}, f32[512]{0:T(512)}, u32[]{:S(2)}) copy-start(f32[512]{0:T(512)} %copy-done.36) | copy-start | bytes 6148
  579.7 15.1 %slice-start = ((s8[16777216]{0:T(1024)(128)(4,1)}), s8[4194304]{0:T(1024)(128)(4,1)S(1)}, s32[]{:S(2)}) async-start(s8[16777216]{0:T(1024)(128)(4,1)} %bitcast.132), calls=%async_computation.6 | async-start | bytes 8388608
  579.8 15.1 %slice-start.1 = ((s8[16777216]{0:T(1024)(128)(4,1)}), s8[4194304]{0:T(1024)(128)(4,1)S(1)}, s32[]{:S(2)}) async-start(s8[16777216]{0:T(1024)(128)(4,1)} %bitcast.132), calls=%async_computation.7 | async-start | bytes 8388608
  579.8 15.1 %slice-start.2 = ((s8[16777216]{0:T(1024)(128)(4,1)}), s8[4194304]{0:T(1024)(128)(4,1)S(1)}, s32[]{:S(2)}) async-start(s8[16777216]{0:T(1024)(128)(4,1)} %bitcast.132), calls=%async_computation.8 | async-start | bytes 8388608
  579.8 16.4 %slice-start.3 = ((s8[16777216]{0:T(1024)(128)(4,1)}), s8[4194304]{0:T(1024)(128)(4,1)S(1)}, s32[]{:S(2)}) async-start(s8[16777216]{0:T(1024)(128)(4,1)} %bitcast.132), calls=%async_computation.9 | async-start | bytes 8388608
  579.8 16.4 %copy-start.26 = (f32[2,8,512]{2,1,0:T(8,128)S(1)}, f32[2,8,512]{2,1,0:T(8,128)}, u32[]{:S(2)}) copy-start(f32[2,8,512]{2,1,0:T(8,128)} %log_add_fusion) | copy-start | bytes 98308
  596.2 11.7 %copy-start.22 = (bf16[512,8,32]{0,2,1:T(8,128)(2,1)S(1)}, bf16[512,8,32]{0,2,1:T(8,128)(2,1)}, u32[]{:S(2)}) copy-start(bf16[512,8,32]{0,2,1:T(8,128)(2,1)} %copy-done.21) | copy-start | bytes 786436
  596.2 11.7 %copy-start.24 = (bf16[512,8,32]{0,2,1:T(8,128)(2,1)S(1)}, bf16[512,8,32]{0,2,1:T(8,128)(2,1)}, u32[]{:S(2)}) copy-start(bf16[512,8,32]{0,2,1:T(8,128)(2,1)} %copy-done.23) | copy-start | bytes 786436
  620.6 5.5 copy-start.25
  625.4 5.6 slice-start.4
  631.0 5.1 copy-start.3
  631.0 8.6 %copy-start.15 = (bf16[1024,1024]{1,0:T(8,128)(2,1)S(1)}, bf16[1024,1024]{1,0:T(8,128)(2,1)}, u32[]{:S(2)}) copy-start(bf16[1024,1024]{1,0:T(8,128)(2,1)} %convolution_convert_fusion.1) | copy-start | bytes 6291460
  738.0 7.3 copy-start.43
  (23 other events, 65.5 us)
Sparse Core Ops, SparseCore 0:
  128.5 79.7 all-gather.2
  210.4 87.9 all-gather.4
  361.6 83.6 reduce-scatter.4
  447.5 77.2 reduce-scatter.2
